TPU v7x, 512 devices: a whole 4x4x16 slice. The times are simulated.
512 devices in a mesh: ctx: 32 (over y, z_lo), head: 16 (over x, z_hi, core).
Axes of the slice: x: 4, y: 4, z: 16 (z_hi: 2, z_lo: 8; z = z_hi * 8 + z_lo), core: 2. Of those that a mesh axis runs over, the one named last changes fastest.
Arguments:
- q_nope: bfloat16 [4096, 8192], P('ctx', 'head'), may hold values from -6 to 6
- q_rope: bfloat16 [4096, 4096], P('ctx', 'head')
- latent: bfloat16 [4096, 512], P('ctx'), may hold values from -6 to 6
- rope_keys: bfloat16 [4096, 64], P('ctx')
- seg_ids: int32 [4096], replicated, may hold values from 0 to 7, never falling along the last dimension, each value on 1 to 3072 neighbouring positions
- w_uk: bfloat16 [512, 8192], P(None, 'head'), may hold values from -0.25 to 0.25
- w_uv: bfloat16 [512, 8192], P(None, 'head'), may hold values from -0.25 to 0.25
- w_out: bfloat16 [8192, 3584], P('head'), may hold values from -0.25 to 0.25
Outputs:
- projected: bfloat16 [4096, 3584], P(('ctx', 'head'))
Inputs may be any that keep to these rules, and one draw needn't show every extreme that they name: `seg_ids`: document number of each token: 8 documents laid end to end, never falling along the window, the longest exactly 3072 tokens.
All inputs are finite; a program needn't handle non-finite values.
Results may differ from a plain program's by a relative error of at most 0.02.
Values may be sent and summed in bfloat16 or wider, within the bound.
A program may use at most 64 MiB of HBM per device.

v0:
```python
import math

import jax
import jax.numpy as jnp
from jax import lax
from jax.sharding import PartitionSpec as P

LAT = 512
NOPE = 128
ROPE = 64
VDIM = 128


def from_behind(block, axis, distance):
    devices = range(lax.axis_size(axis))
    route = [(i - distance, i) for i in devices if i - distance in devices]
    return lax.ppermute(block, axis, route)


def body(q_nope, q_rope, latent, rope_keys, seg_ids, w_uk, w_uv, w_out):
    tok_rows = latent.shape[0]
    head_count = q_nope.shape[1] // NOPE
    soft_scale = 1.0 / math.sqrt(NOPE + ROPE)
    my_index = lax.axis_index("ctx")
    first_row = my_index * tok_rows
    query_pos = first_row + jnp.arange(tok_rows, dtype=jnp.int32)
    query_seg = lax.dynamic_slice_in_dim(seg_ids, first_row, tok_rows)
    absorbed = jnp.einsum(
        "thn,chn->htc",
        q_nope.reshape(tok_rows, head_count, NOPE),
        w_uk.reshape(LAT, head_count, NOPE),
        preferred_element_type=jnp.float32,
    ).astype(jnp.bfloat16)
    absorbed = absorbed.reshape(head_count * tok_rows, LAT)
    rotated = (
        q_rope.reshape(tok_rows, head_count, ROPE)
        .transpose(1, 0, 2)
        .reshape(head_count * tok_rows, ROPE)
    )
    row_pos = jnp.tile(query_pos, head_count)
    row_seg = jnp.tile(query_seg, head_count)

    def attend(carried, incoming, begin_at):
        lat_block, rope_block = incoming
        amount = lat_block.shape[0]
        key_pos = begin_at + jnp.arange(amount, dtype=jnp.int32)
        key_seg = lax.dynamic_slice_in_dim(seg_ids, begin_at, amount)

        def update(previous):
            old_max, old_sum, old_acc = previous
            scores = jnp.dot(absorbed, lat_block.T, preferred_element_type=jnp.float32)
            scores = (
                scores + jnp.dot(rotated, rope_block.T, preferred_element_type=jnp.float32)
            ) * soft_scale
            visible = (key_seg[None, :] == row_seg[:, None]) & (
                key_pos[None, :] <= row_pos[:, None]
            )
            block_max = jnp.max(jnp.where(visible, scores, -jnp.inf), axis=1)
            new_max = jnp.maximum(old_max, block_max)
            safe_max = jnp.where(jnp.isfinite(new_max), new_max, 0.0)
            powers = jnp.where(visible, jnp.exp(scores - safe_max[:, None]), 0.0)
            shrink = jnp.exp(old_max - safe_max)
            new_sum = old_sum * shrink + jnp.sum(powers, axis=1)
            new_acc = old_acc * shrink[:, None] + jnp.dot(
                powers.astype(jnp.bfloat16), lat_block, preferred_element_type=jnp.float32
            )
            return (new_max, new_sum, new_acc)

        active = (begin_at <= query_pos[-1]) & (key_seg[-1] >= query_seg[0])
        return lax.cond(active, update, lambda previous: previous, carried)

    query_total = head_count * tok_rows
    initial = (
        jnp.full((query_total,), -jnp.inf, jnp.float32),
        jnp.zeros((query_total,), jnp.float32),
        jnp.zeros((query_total, LAT), jnp.float32),
    )
    axis_size = lax.axis_size("ctx")

    def advance(hop_index, both):
        carried, key_block = both
        source = (my_index - hop_index) % axis_size
        carried = attend(carried, key_block, source * tok_rows)
        key_block = from_behind((key_block[0], key_block[1]), "ctx", 1)
        return (carried, key_block)

    carried, key_block = lax.fori_loop(0, axis_size - 1, advance, (initial, (latent, rope_keys)))
    last_source = (my_index - (axis_size - 1)) % axis_size
    carried = attend(carried, key_block, last_source * tok_rows)
    final_max, final_sum, final_acc = carried
    latent_context = (
        (final_acc / final_sum[:, None]).astype(jnp.bfloat16).reshape(head_count, tok_rows, LAT)
    )
    head_out = jnp.einsum(
        "htc,chv->thv",
        latent_context,
        w_uv.reshape(LAT, head_count, VDIM),
        preferred_element_type=jnp.float32,
    ).astype(jnp.bfloat16)
    head_out = head_out.reshape(tok_rows, head_count * VDIM)
    return lax.psum_scatter(
        jnp.dot(head_out, w_out, preferred_element_type=jnp.float32).astype(jnp.bfloat16),
        "head",
        scatter_dimension=0,
        tiled=True,
    )


def solution(mesh):
    placed = (
        P("ctx", "head"),
        P("ctx", "head"),
        P("ctx", None),
        P("ctx", None),
        P(),
        P(None, "head"),
        P(None, "head"),
        P("head", None),
    )
    return jax.shard_map(
        body, mesh=mesh, in_specs=placed, out_specs=P(("ctx", "head"), None), check_vma=False
    )
```

profile of v0, /device:TPU:24, one launch (start us, length us, event | category | flops | bytes accessed | tf_op | source)
XLA Modules:
  0.0 655.5 jit_solution(15953207170778486790)
XLA Ops:
  14.4 520.7 %while.25 = (s32[]{:T(128)}, f32[512]{0:T(512)S(1)}, f32[512]{0:T(512)S(1)}, f32[512,512]{1,0:T(8,128)S(1)}, bf16[128,512]{1,0:T(8,128)(2,1)S(1)}, /*index=5*/bf...) while((s32[]{:T(128)}, f32[512]{0:T(512)S(1)}, ...), condition=%wide.region_5.6_spmd.clone.clone, body=%wide.region_0.5_spmd.clone.clone.sunk | while | flops 144379024 | bytes 5219430 | solution.py:87
  26.5 3.9 conditional.6
  36.3 4.2 collective-permute-start.1
  43.6 3.9 conditional.6
  59.5 3.9 conditional.6
  74.7 3.9 conditional.6
  78.6 4.6 collective-permute-done.1
  91.4 3.9 conditional.6
  95.3 4.6 collective-permute-done.1
  112.0 4.6 collective-permute-done.1
  124.8 3.9 conditional.6
  128.7 4.6 collective-permute-done.1
  141.5 3.9 conditional.6
  145.4 4.6 collective-permute-done.1
  158.2 3.9 conditional.6
  162.1 4.6 collective-permute-done.1
  178.8 4.6 collective-permute-done.1
  191.6 3.9 conditional.6
  195.5 4.6 collective-permute-done.1
  208.3 3.9 conditional.6
  212.2 4.6 collective-permute-done.1
  225.0 3.9 conditional.6
  228.9 4.6 collective-permute-done.1
  245.6 4.9 collective-permute-done.1
  258.7 3.9 conditional.6
  262.6 5.0 collective-permute-done.1
  279.7 4.6 collective-permute-done.1
  292.5 3.9 conditional.6
  296.4 4.6 collective-permute-done.1
  309.2 3.9 conditional.6
  313.1 4.6 collective-permute-done.1
  325.9 3.9 conditional.6
  329.8 4.6 collective-permute-done.1
  346.5 4.6 collective-permute-done.1
  359.3 3.9 conditional.6
  363.2 4.6 collective-permute-done.1
  376.0 3.9 conditional.6
  379.9 4.6 collective-permute-done.1
  392.7 8.5 %collective-permute-done.1 = bf16[128,64]{1,0:T(8,128)(2,1)S(1)} collective-permute-done((bf16[128,64]{1,0:T(8,128)(2,1)}, bf16[128,64]{1,0:T(8,128)(2,1)S(1)}, u32[]{:S(2)}, u32[]{:S(2)}) %collective-permute-start.1) | collective-permute-done | bytes 16416 | tf_op jit(solution)/shard_map/while/body/eval_jaxpr/ppermute | solution.py:17
  409.4 8.5 %collective-permute-done.1 = bf16[128,64]{1,0:T(8,128)(2,1)S(1)} collective-permute-done((bf16[128,64]{1,0:T(8,128)(2,1)}, bf16[128,64]{1,0:T(8,128)(2,1)S(1)}, u32[]{:S(2)}, u32[]{:S(2)}) %collective-permute-start.1) | collective-permute-done | bytes 16416 | tf_op jit(solution)/shard_map/while/body/eval_jaxpr/ppermute | solution.py:17
  426.1 8.5 %collective-permute-done.1 = bf16[128,64]{1,0:T(8,128)(2,1)S(1)} collective-permute-done((bf16[128,64]{1,0:T(8,128)(2,1)}, bf16[128,64]{1,0:T(8,128)(2,1)S(1)}, u32[]{:S(2)}, u32[]{:S(2)}) %collective-permute-start.1) | collective-permute-done | bytes 16416 | tf_op jit(solution)/shard_map/while/body/eval_jaxpr/ppermute | solution.py:17
  442.8 8.5 %collective-permute-done.1 = bf16[128,64]{1,0:T(8,128)(2,1)S(1)} collective-permute-done((bf16[128,64]{1,0:T(8,128)(2,1)}, bf16[128,64]{1,0:T(8,128)(2,1)S(1)}, u32[]{:S(2)}, u32[]{:S(2)}) %collective-permute-start.1) | collective-permute-done | bytes 16416 | tf_op jit(solution)/shard_map/while/body/eval_jaxpr/ppermute | solution.py:17
  459.5 8.5 %collective-permute-done.1 = bf16[128,64]{1,0:T(8,128)(2,1)S(1)} collective-permute-done((bf16[128,64]{1,0:T(8,128)(2,1)}, bf16[128,64]{1,0:T(8,128)(2,1)S(1)}, u32[]{:S(2)}, u32[]{:S(2)}) %collective-permute-start.1) | collective-permute-done | bytes 16416 | tf_op jit(solution)/shard_map/while/body/eval_jaxpr/ppermute | solution.py:17
  476.2 8.5 %collective-permute-done.1 = bf16[128,64]{1,0:T(8,128)(2,1)S(1)} collective-permute-done((bf16[128,64]{1,0:T(8,128)(2,1)}, bf16[128,64]{1,0:T(8,128)(2,1)S(1)}, u32[]{:S(2)}, u32[]{:S(2)}) %collective-permute-start.1) | collective-permute-done | bytes 16416 | tf_op jit(solution)/shard_map/while/body/eval_jaxpr/ppermute | solution.py:17
  492.9 8.8 %collective-permute-done.1 = bf16[128,64]{1,0:T(8,128)(2,1)S(1)} collective-permute-done((bf16[128,64]{1,0:T(8,128)(2,1)}, bf16[128,64]{1,0:T(8,128)(2,1)S(1)}, u32[]{:S(2)}, u32[]{:S(2)}) %collective-permute-start.1) | collective-permute-done | bytes 16416 | tf_op jit(solution)/shard_map/while/body/eval_jaxpr/ppermute | solution.py:17
  509.9 8.5 %collective-permute-done.1 = bf16[128,64]{1,0:T(8,128)(2,1)S(1)} collective-permute-done((bf16[128,64]{1,0:T(8,128)(2,1)}, bf16[128,64]{1,0:T(8,128)(2,1)S(1)}, u32[]{:S(2)}, u32[]{:S(2)}) %collective-permute-start.1) | collective-permute-done | bytes 16416 | tf_op jit(solution)/shard_map/while/body/eval_jaxpr/ppermute | solution.py:17
  526.6 8.5 %collective-permute-done.1 = bf16[128,64]{1,0:T(8,128)(2,1)S(1)} collective-permute-done((bf16[128,64]{1,0:T(8,128)(2,1)}, bf16[128,64]{1,0:T(8,128)(2,1)S(1)}, u32[]{:S(2)}, u32[]{:S(2)}) %collective-permute-start.1) | collective-permute-done | bytes 16416 | tf_op jit(solution)/shard_map/while/body/eval_jaxpr/ppermute | solution.py:17
  539.2 109.4 %reduce-scatter.2.cloned.1.call-done = bf16[8,3584]{1,0:T(8,128)(2,1)} async-done(((bf16[128,3584]{1,0:T(8,128)(2,1)}), bf16[8,3584]{1,0:T(8,128)(2,1)}) %reduce-scatter.2.cloned.1.call-update) | async-done | bytes 57360 | tf_op jit(solution)/shard_map/reduce_scatter | solution.py:101
  (516 shorter events, 342.9 us)
Async XLA Ops:
  6.5 642.1 %reduce-scatter.2.cloned.1.call-start = ((), (), s32[]{:S(2)}) async-start(), calls=%async_computation.1 | async-start | bytes 974848 | tf_op jit(solution)/shard_map/reduce_scatter | solution.py:101
  15.1 18.0 %collective-permute-start = (bf16[128,512]{1,0:T(8,128)(2,1)}, bf16[128,512]{1,0:T(8,128)(2,1)S(1)}, u32[]{:S(2)}, u32[]{:S(2)}) collective-permute-start(bf16[128,512]{1,0:T(8,128)(2,1)} %copy.58), channel_id=1, source_target_pairs={{0,16},{16,32},{32,48},{48,64},{64,80},{80,96},{96,112},{112,128},... | collective-permute-start | bytes 393224 | tf_op jit(solution)/shard_map/while/body/eval_jaxpr/ppermute | solution.py:17
  19.5 13.5 %collective-permute-start.1 = (bf16[128,64]{1,0:T(8,128)(2,1)}, bf16[128,64]{1,0:T(8,128)(2,1)S(1)}, u32[]{:S(2)}, u32[]{:S(2)}) collective-permute-start(bf16[128,64]{1,0:T(8,128)(2,1)} %copy.59), channel_id=1, source_target_pairs={{0,16},{16,32},{32,48},{48,64},{64,80},{80,96},{96,112},{112,128},... | collective-permute-start | bytes 49160 | tf_op jit(solution)/shard_map/while/body/eval_jaxpr/ppermute | solution.py:17
  33.7 16.0 %collective-permute-start = (bf16[128,512]{1,0:T(8,128)(2,1)}, bf16[128,512]{1,0:T(8,128)(2,1)S(1)}, u32[]{:S(2)}, u32[]{:S(2)}) collective-permute-start(bf16[128,512]{1,0:T(8,128)(2,1)} %copy.58), channel_id=1, source_target_pairs={{0,16},{16,32},{32,48},{48,64},{64,80},{80,96},{96,112},{112,128},... | collective-permute-start | bytes 393224 | tf_op jit(solution)/shard_map/while/body/eval_jaxpr/ppermute | solution.py:17
  36.3 13.5 %collective-permute-start.1 = (bf16[128,64]{1,0:T(8,128)(2,1)}, bf16[128,64]{1,0:T(8,128)(2,1)S(1)}, u32[]{:S(2)}, u32[]{:S(2)}) collective-permute-start(bf16[128,64]{1,0:T(8,128)(2,1)} %copy.59), channel_id=1, source_target_pairs={{0,16},{16,32},{32,48},{48,64},{64,80},{80,96},{96,112},{112,128},... | collective-permute-start | bytes 49160 | tf_op jit(solution)/shard_map/while/body/eval_jaxpr/ppermute | solution.py:17
  50.4 16.0 %collective-permute-start = (bf16[128,512]{1,0:T(8,128)(2,1)}, bf16[128,512]{1,0:T(8,128)(2,1)S(1)}, u32[]{:S(2)}, u32[]{:S(2)}) collective-permute-start(bf16[128,512]{1,0:T(8,128)(2,1)} %copy.58), channel_id=1, source_target_pairs={{0,16},{16,32},{32,48},{48,64},{64,80},{80,96},{96,112},{112,128},... | collective-permute-start | bytes 393224 | tf_op jit(solution)/shard_map/while/body/eval_jaxpr/ppermute | solution.py:17
  67.1 16.0 %collective-permute-start = (bf16[128,512]{1,0:T(8,128)(2,1)}, bf16[128,512]{1,0:T(8,128)(2,1)S(1)}, u32[]{:S(2)}, u32[]{:S(2)}) collective-permute-start(bf16[128,512]{1,0:T(8,128)(2,1)} %copy.58), channel_id=1, source_target_pairs={{0,16},{16,32},{32,48},{48,64},{64,80},{80,96},{96,112},{112,128},... | collective-permute-start | bytes 393224 | tf_op jit(solution)/shard_map/while/body/eval_jaxpr/ppermute | solution.py:17
  69.7 13.5 %collective-permute-start.1 = (bf16[128,64]{1,0:T(8,128)(2,1)}, bf16[128,64]{1,0:T(8,128)(2,1)S(1)}, u32[]{:S(2)}, u32[]{:S(2)}) collective-permute-start(bf16[128,64]{1,0:T(8,128)(2,1)} %copy.59), channel_id=1, source_target_pairs={{0,16},{16,32},{32,48},{48,64},{64,80},{80,96},{96,112},{112,128},... | collective-permute-start | bytes 49160 | tf_op jit(solution)/shard_map/while/body/eval_jaxpr/ppermute | solution.py:17
  83.8 16.0 %collective-permute-start = (bf16[128,512]{1,0:T(8,128)(2,1)}, bf16[128,512]{1,0:T(8,128)(2,1)S(1)}, u32[]{:S(2)}, u32[]{:S(2)}) collective-permute-start(bf16[128,512]{1,0:T(8,128)(2,1)} %copy.58), channel_id=1, source_target_pairs={{0,16},{16,32},{32,48},{48,64},{64,80},{80,96},{96,112},{112,128},... | collective-permute-start | bytes 393224 | tf_op jit(solution)/shard_map/while/body/eval_jaxpr/ppermute | solution.py:17
  86.4 13.5 %collective-permute-start.1 = (bf16[128,64]{1,0:T(8,128)(2,1)}, bf16[128,64]{1,0:T(8,128)(2,1)S(1)}, u32[]{:S(2)}, u32[]{:S(2)}) collective-permute-start(bf16[128,64]{1,0:T(8,128)(2,1)} %copy.59), channel_id=1, source_target_pairs={{0,16},{16,32},{32,48},{48,64},{64,80},{80,96},{96,112},{112,128},... | collective-permute-start | bytes 49160 | tf_op jit(solution)/shard_map/while/body/eval_jaxpr/ppermute | solution.py:17
  100.5 16.0 %collective-permute-start = (bf16[128,512]{1,0:T(8,128)(2,1)}, bf16[128,512]{1,0:T(8,128)(2,1)S(1)}, u32[]{:S(2)}, u32[]{:S(2)}) collective-permute-start(bf16[128,512]{1,0:T(8,128)(2,1)} %copy.58), channel_id=1, source_target_pairs={{0,16},{16,32},{32,48},{48,64},{64,80},{80,96},{96,112},{112,128},... | collective-permute-start | bytes 393224 | tf_op jit(solution)/shard_map/while/body/eval_jaxpr/ppermute | solution.py:17
  103.1 13.5 %collective-permute-start.1 = (bf16[128,64]{1,0:T(8,128)(2,1)}, bf16[128,64]{1,0:T(8,128)(2,1)S(1)}, u32[]{:S(2)}, u32[]{:S(2)}) collective-permute-start(bf16[128,64]{1,0:T(8,128)(2,1)} %copy.59), channel_id=1, source_target_pairs={{0,16},{16,32},{32,48},{48,64},{64,80},{80,96},{96,112},{112,128},... | collective-permute-start | bytes 49160 | tf_op jit(solution)/shard_map/while/body/eval_jaxpr/ppermute | solution.py:17
  117.2 16.0 %collective-permute-start = (bf16[128,512]{1,0:T(8,128)(2,1)}, bf16[128,512]{1,0:T(8,128)(2,1)S(1)}, u32[]{:S(2)}, u32[]{:S(2)}) collective-permute-start(bf16[128,512]{1,0:T(8,128)(2,1)} %copy.58), channel_id=1, source_target_pairs={{0,16},{16,32},{32,48},{48,64},{64,80},{80,96},{96,112},{112,128},... | collective-permute-start | bytes 393224 | tf_op jit(solution)/shard_map/while/body/eval_jaxpr/ppermute | solution.py:17
  119.8 13.5 %collective-permute-start.1 = (bf16[128,64]{1,0:T(8,128)(2,1)}, bf16[128,64]{1,0:T(8,128)(2,1)S(1)}, u32[]{:S(2)}, u32[]{:S(2)}) collective-permute-start(bf16[128,64]{1,0:T(8,128)(2,1)} %copy.59), channel_id=1, source_target_pairs={{0,16},{16,32},{32,48},{48,64},{64,80},{80,96},{96,112},{112,128},... | collective-permute-start | bytes 49160 | tf_op jit(solution)/shard_map/while/body/eval_jaxpr/ppermute | solution.py:17
  133.9 16.0 %collective-permute-start = (bf16[128,512]{1,0:T(8,128)(2,1)}, bf16[128,512]{1,0:T(8,128)(2,1)S(1)}, u32[]{:S(2)}, u32[]{:S(2)}) collective-permute-start(bf16[128,512]{1,0:T(8,128)(2,1)} %copy.58), channel_id=1, source_target_pairs={{0,16},{16,32},{32,48},{48,64},{64,80},{80,96},{96,112},{112,128},... | collective-permute-start | bytes 393224 | tf_op jit(solution)/shard_map/while/body/eval_jaxpr/ppermute | solution.py:17
  150.6 16.0 %collective-permute-start = (bf16[128,512]{1,0:T(8,128)(2,1)}, bf16[128,512]{1,0:T(8,128)(2,1)S(1)}, u32[]{:S(2)}, u32[]{:S(2)}) collective-permute-start(bf16[128,512]{1,0:T(8,128)(2,1)} %copy.58), channel_id=1, source_target_pairs={{0,16},{16,32},{32,48},{48,64},{64,80},{80,96},{96,112},{112,128},... | collective-permute-start | bytes 393224 | tf_op jit(solution)/shard_map/while/body/eval_jaxpr/ppermute | solution.py:17
  153.2 13.5 %collective-permute-start.1 = (bf16[128,64]{1,0:T(8,128)(2,1)}, bf16[128,64]{1,0:T(8,128)(2,1)S(1)}, u32[]{:S(2)}, u32[]{:S(2)}) collective-permute-start(bf16[128,64]{1,0:T(8,128)(2,1)} %copy.59), channel_id=1, source_target_pairs={{0,16},{16,32},{32,48},{48,64},{64,80},{80,96},{96,112},{112,128},... | collective-permute-start | bytes 49160 | tf_op jit(solution)/shard_map/while/body/eval_jaxpr/ppermute | solution.py:17
  167.3 16.0 %collective-permute-start = (bf16[128,512]{1,0:T(8,128)(2,1)}, bf16[128,512]{1,0:T(8,128)(2,1)S(1)}, u32[]{:S(2)}, u32[]{:S(2)}) collective-permute-start(bf16[128,512]{1,0:T(8,128)(2,1)} %copy.58), channel_id=1, source_target_pairs={{0,16},{16,32},{32,48},{48,64},{64,80},{80,96},{96,112},{112,128},... | collective-permute-start | bytes 393224 | tf_op jit(solution)/shard_map/while/body/eval_jaxpr/ppermute | solution.py:17
  169.9 13.5 %collective-permute-start.1 = (bf16[128,64]{1,0:T(8,128)(2,1)}, bf16[128,64]{1,0:T(8,128)(2,1)S(1)}, u32[]{:S(2)}, u32[]{:S(2)}) collective-permute-start(bf16[128,64]{1,0:T(8,128)(2,1)} %copy.59), channel_id=1, source_target_pairs={{0,16},{16,32},{32,48},{48,64},{64,80},{80,96},{96,112},{112,128},... | collective-permute-start | bytes 49160 | tf_op jit(solution)/shard_map/while/body/eval_jaxpr/ppermute | solution.py:17
  184.0 16.0 %collective-permute-start = (bf16[128,512]{1,0:T(8,128)(2,1)}, bf16[128,512]{1,0:T(8,128)(2,1)S(1)}, u32[]{:S(2)}, u32[]{:S(2)}) collective-permute-start(bf16[128,512]{1,0:T(8,128)(2,1)} %copy.58), channel_id=1, source_target_pairs={{0,16},{16,32},{32,48},{48,64},{64,80},{80,96},{96,112},{112,128},... | collective-permute-start | bytes 393224 | tf_op jit(solution)/shard_map/while/body/eval_jaxpr/ppermute | solution.py:17
  200.7 16.0 %collective-permute-start = (bf16[128,512]{1,0:T(8,128)(2,1)}, bf16[128,512]{1,0:T(8,128)(2,1)S(1)}, u32[]{:S(2)}, u32[]{:S(2)}) collective-permute-start(bf16[128,512]{1,0:T(8,128)(2,1)} %copy.58), channel_id=1, source_target_pairs={{0,16},{16,32},{32,48},{48,64},{64,80},{80,96},{96,112},{112,128},... | collective-permute-start | bytes 393224 | tf_op jit(solution)/shard_map/while/body/eval_jaxpr/ppermute | solution.py:17
  203.3 13.5 %collective-permute-start.1 = (bf16[128,64]{1,0:T(8,128)(2,1)}, bf16[128,64]{1,0:T(8,128)(2,1)S(1)}, u32[]{:S(2)}, u32[]{:S(2)}) collective-permute-start(bf16[128,64]{1,0:T(8,128)(2,1)} %copy.59), channel_id=1, source_target_pairs={{0,16},{16,32},{32,48},{48,64},{64,80},{80,96},{96,112},{112,128},... | collective-permute-start | bytes 49160 | tf_op jit(solution)/shard_map/while/body/eval_jaxpr/ppermute | solution.py:17
  217.4 16.0 %collective-permute-start = (bf16[128,512]{1,0:T(8,128)(2,1)}, bf16[128,512]{1,0:T(8,128)(2,1)S(1)}, u32[]{:S(2)}, u32[]{:S(2)}) collective-permute-start(bf16[128,512]{1,0:T(8,128)(2,1)} %copy.58), channel_id=1, source_target_pairs={{0,16},{16,32},{32,48},{48,64},{64,80},{80,96},{96,112},{112,128},... | collective-permute-start | bytes 393224 | tf_op jit(solution)/shard_map/while/body/eval_jaxpr/ppermute | solution.py:17
  220.0 13.5 %collective-permute-start.1 = (bf16[128,64]{1,0:T(8,128)(2,1)}, bf16[128,64]{1,0:T(8,128)(2,1)S(1)}, u32[]{:S(2)}, u32[]{:S(2)}) collective-permute-start(bf16[128,64]{1,0:T(8,128)(2,1)} %copy.59), channel_id=1, source_target_pairs={{0,16},{16,32},{32,48},{48,64},{64,80},{80,96},{96,112},{112,128},... | collective-permute-start | bytes 49160 | tf_op jit(solution)/shard_map/while/body/eval_jaxpr/ppermute | solution.py:17
  234.1 16.3 %collective-permute-start = (bf16[128,512]{1,0:T(8,128)(2,1)}, bf16[128,512]{1,0:T(8,128)(2,1)S(1)}, u32[]{:S(2)}, u32[]{:S(2)}) collective-permute-start(bf16[128,512]{1,0:T(8,128)(2,1)} %copy.58), channel_id=1, source_target_pairs={{0,16},{16,32},{32,48},{48,64},{64,80},{80,96},{96,112},{112,128},... | collective-permute-start | bytes 393224 | tf_op jit(solution)/shard_map/while/body/eval_jaxpr/ppermute | solution.py:17
  236.7 13.8 %collective-permute-start.1 = (bf16[128,64]{1,0:T(8,128)(2,1)}, bf16[128,64]{1,0:T(8,128)(2,1)S(1)}, u32[]{:S(2)}, u32[]{:S(2)}) collective-permute-start(bf16[128,64]{1,0:T(8,128)(2,1)} %copy.59), channel_id=1, source_target_pairs={{0,16},{16,32},{32,48},{48,64},{64,80},{80,96},{96,112},{112,128},... | collective-permute-start | bytes 49160 | tf_op jit(solution)/shard_map/while/body/eval_jaxpr/ppermute | solution.py:17
  251.1 16.5 %collective-permute-start = (bf16[128,512]{1,0:T(8,128)(2,1)}, bf16[128,512]{1,0:T(8,128)(2,1)S(1)}, u32[]{:S(2)}, u32[]{:S(2)}) collective-permute-start(bf16[128,512]{1,0:T(8,128)(2,1)} %copy.58), channel_id=1, source_target_pairs={{0,16},{16,32},{32,48},{48,64},{64,80},{80,96},{96,112},{112,128},... | collective-permute-start | bytes 393224 | tf_op jit(solution)/shard_map/while/body/eval_jaxpr/ppermute | solution.py:17
  253.7 13.9 %collective-permute-start.1 = (bf16[128,64]{1,0:T(8,128)(2,1)}, bf16[128,64]{1,0:T(8,128)(2,1)S(1)}, u32[]{:S(2)}, u32[]{:S(2)}) collective-permute-start(bf16[128,64]{1,0:T(8,128)(2,1)} %copy.59), channel_id=1, source_target_pairs={{0,16},{16,32},{32,48},{48,64},{64,80},{80,96},{96,112},{112,128},... | collective-permute-start | bytes 49160 | tf_op jit(solution)/shard_map/while/body/eval_jaxpr/ppermute | solution.py:17
  268.2 16.0 %collective-permute-start = (bf16[128,512]{1,0:T(8,128)(2,1)}, bf16[128,512]{1,0:T(8,128)(2,1)S(1)}, u32[]{:S(2)}, u32[]{:S(2)}) collective-permute-start(bf16[128,512]{1,0:T(8,128)(2,1)} %copy.58), channel_id=1, source_target_pairs={{0,16},{16,32},{32,48},{48,64},{64,80},{80,96},{96,112},{112,128},... | collective-permute-start | bytes 393224 | tf_op jit(solution)/shard_map/while/body/eval_jaxpr/ppermute | solution.py:17
  284.9 16.0 %collective-permute-start = (bf16[128,512]{1,0:T(8,128)(2,1)}, bf16[128,512]{1,0:T(8,128)(2,1)S(1)}, u32[]{:S(2)}, u32[]{:S(2)}) collective-permute-start(bf16[128,512]{1,0:T(8,128)(2,1)} %copy.58), channel_id=1, source_target_pairs={{0,16},{16,32},{32,48},{48,64},{64,80},{80,96},{96,112},{112,128},... | collective-permute-start | bytes 393224 | tf_op jit(solution)/shard_map/while/body/eval_jaxpr/ppermute | solution.py:17
  287.5 13.5 %collective-permute-start.1 = (bf16[128,64]{1,0:T(8,128)(2,1)}, bf16[128,64]{1,0:T(8,128)(2,1)S(1)}, u32[]{:S(2)}, u32[]{:S(2)}) collective-permute-start(bf16[128,64]{1,0:T(8,128)(2,1)} %copy.59), channel_id=1, source_target_pairs={{0,16},{16,32},{32,48},{48,64},{64,80},{80,96},{96,112},{112,128},... | collective-permute-start | bytes 49160 | tf_op jit(solution)/shard_map/while/body/eval_jaxpr/ppermute | solution.py:17
  301.6 16.0 %collective-permute-start = (bf16[128,512]{1,0:T(8,128)(2,1)}, bf16[128,512]{1,0:T(8,128)(2,1)S(1)}, u32[]{:S(2)}, u32[]{:S(2)}) collective-permute-start(bf16[128,512]{1,0:T(8,128)(2,1)} %copy.58), channel_id=1, source_target_pairs={{0,16},{16,32},{32,48},{48,64},{64,80},{80,96},{96,112},{112,128},... | collective-permute-start | bytes 393224 | tf_op jit(solution)/shard_map/while/body/eval_jaxpr/ppermute | solution.py:17
  304.2 13.5 %collective-permute-start.1 = (bf16[128,64]{1,0:T(8,128)(2,1)}, bf16[128,64]{1,0:T(8,128)(2,1)S(1)}, u32[]{:S(2)}, u32[]{:S(2)}) collective-permute-start(bf16[128,64]{1,0:T(8,128)(2,1)} %copy.59), channel_id=1, source_target_pairs={{0,16},{16,32},{32,48},{48,64},{64,80},{80,96},{96,112},{112,128},... | collective-permute-start | bytes 49160 | tf_op jit(solution)/shard_map/while/body/eval_jaxpr/ppermute | solution.py:17
  318.4 16.0 %collective-permute-start = (bf16[128,512]{1,0:T(8,128)(2,1)}, bf16[128,512]{1,0:T(8,128)(2,1)S(1)}, u32[]{:S(2)}, u32[]{:S(2)}) collective-permute-start(bf16[128,512]{1,0:T(8,128)(2,1)} %copy.58), channel_id=1, source_target_pairs={{0,16},{16,32},{32,48},{48,64},{64,80},{80,96},{96,112},{112,128},... | collective-permute-start | bytes 393224 | tf_op jit(solution)/shard_map/while/body/eval_jaxpr/ppermute | solution.py:17
  335.1 16.0 %collective-permute-start = (bf16[128,512]{1,0:T(8,128)(2,1)}, bf16[128,512]{1,0:T(8,128)(2,1)S(1)}, u32[]{:S(2)}, u32[]{:S(2)}) collective-permute-start(bf16[128,512]{1,0:T(8,128)(2,1)} %copy.58), channel_id=1, source_target_pairs={{0,16},{16,32},{32,48},{48,64},{64,80},{80,96},{96,112},{112,128},... | collective-permute-start | bytes 393224 | tf_op jit(solution)/shard_map/while/body/eval_jaxpr/ppermute | solution.py:17
  337.6 13.5 %collective-permute-start.1 = (bf16[128,64]{1,0:T(8,128)(2,1)}, bf16[128,64]{1,0:T(8,128)(2,1)S(1)}, u32[]{:S(2)}, u32[]{:S(2)}) collective-permute-start(bf16[128,64]{1,0:T(8,128)(2,1)} %copy.59), channel_id=1, source_target_pairs={{0,16},{16,32},{32,48},{48,64},{64,80},{80,96},{96,112},{112,128},... | collective-permute-start | bytes 49160 | tf_op jit(solution)/shard_map/while/body/eval_jaxpr/ppermute | solution.py:17
  351.8 16.0 %collective-permute-start = (bf16[128,512]{1,0:T(8,128)(2,1)}, bf16[128,512]{1,0:T(8,128)(2,1)S(1)}, u32[]{:S(2)}, u32[]{:S(2)}) collective-permute-start(bf16[128,512]{1,0:T(8,128)(2,1)} %copy.58), channel_id=1, source_target_pairs={{0,16},{16,32},{32,48},{48,64},{64,80},{80,96},{96,112},{112,128},... | collective-permute-start | bytes 393224 | tf_op jit(solution)/shard_map/while/body/eval_jaxpr/ppermute | solution.py:17
  368.5 16.0 %collective-permute-start = (bf16[128,512]{1,0:T(8,128)(2,1)}, bf16[128,512]{1,0:T(8,128)(2,1)S(1)}, u32[]{:S(2)}, u32[]{:S(2)}) collective-permute-start(bf16[128,512]{1,0:T(8,128)(2,1)} %copy.58), channel_id=1, source_target_pairs={{0,16},{16,32},{32,48},{48,64},{64,80},{80,96},{96,112},{112,128},... | collective-permute-start | bytes 393224 | tf_op jit(solution)/shard_map/while/body/eval_jaxpr/ppermute | solution.py:17
  385.2 16.0 %collective-permute-start = (bf16[128,512]{1,0:T(8,128)(2,1)}, bf16[128,512]{1,0:T(8,128)(2,1)S(1)}, u32[]{:S(2)}, u32[]{:S(2)}) collective-permute-start(bf16[128,512]{1,0:T(8,128)(2,1)} %copy.58), channel_id=1, source_target_pairs={{0,16},{16,32},{32,48},{48,64},{64,80},{80,96},{96,112},{112,128},... | collective-permute-start | bytes 393224 | tf_op jit(solution)/shard_map/while/body/eval_jaxpr/ppermute | solution.py:17
  401.9 16.0 %collective-permute-start = (bf16[128,512]{1,0:T(8,128)(2,1)}, bf16[128,512]{1,0:T(8,128)(2,1)S(1)}, u32[]{:S(2)}, u32[]{:S(2)}) collective-permute-start(bf16[128,512]{1,0:T(8,128)(2,1)} %copy.58), channel_id=1, source_target_pairs={{0,16},{16,32},{32,48},{48,64},{64,80},{80,96},{96,112},{112,128},... | collective-permute-start | bytes 393224 | tf_op jit(solution)/shard_map/while/body/eval_jaxpr/ppermute | solution.py:17
  418.6 16.0 %collective-permute-start = (bf16[128,512]{1,0:T(8,128)(2,1)}, bf16[128,512]{1,0:T(8,128)(2,1)S(1)}, u32[]{:S(2)}, u32[]{:S(2)}) collective-permute-start(bf16[128,512]{1,0:T(8,128)(2,1)} %copy.58), channel_id=1, source_target_pairs={{0,16},{16,32},{32,48},{48,64},{64,80},{80,96},{96,112},{112,128},... | collective-permute-start | bytes 393224 | tf_op jit(solution)/shard_map/while/body/eval_jaxpr/ppermute | solution.py:17
  435.3 16.0 %collective-permute-start = (bf16[128,512]{1,0:T(8,128)(2,1)}, bf16[128,512]{1,0:T(8,128)(2,1)S(1)}, u32[]{:S(2)}, u32[]{:S(2)}) collective-permute-start(bf16[128,512]{1,0:T(8,128)(2,1)} %copy.58), channel_id=1, source_target_pairs={{0,16},{16,32},{32,48},{48,64},{64,80},{80,96},{96,112},{112,128},... | collective-permute-start | bytes 393224 | tf_op jit(solution)/shard_map/while/body/eval_jaxpr/ppermute | solution.py:17
  452.0 16.0 %collective-permute-start = (bf16[128,512]{1,0:T(8,128)(2,1)}, bf16[128,512]{1,0:T(8,128)(2,1)S(1)}, u32[]{:S(2)}, u32[]{:S(2)}) collective-permute-start(bf16[128,512]{1,0:T(8,128)(2,1)} %copy.58), channel_id=1, source_target_pairs={{0,16},{16,32},{32,48},{48,64},{64,80},{80,96},{96,112},{112,128},... | collective-permute-start | bytes 393224 | tf_op jit(solution)/shard_map/while/body/eval_jaxpr/ppermute | solution.py:17
  468.7 16.0 %collective-permute-start = (bf16[128,512]{1,0:T(8,128)(2,1)}, bf16[128,512]{1,0:T(8,128)(2,1)S(1)}, u32[]{:S(2)}, u32[]{:S(2)}) collective-permute-start(bf16[128,512]{1,0:T(8,128)(2,1)} %copy.58), channel_id=1, source_target_pairs={{0,16},{16,32},{32,48},{48,64},{64,80},{80,96},{96,112},{112,128},... | collective-permute-start | bytes 393224 | tf_op jit(solution)/shard_map/while/body/eval_jaxpr/ppermute | solution.py:17
  485.4 16.3 %collective-permute-start = (bf16[128,512]{1,0:T(8,128)(2,1)}, bf16[128,512]{1,0:T(8,128)(2,1)S(1)}, u32[]{:S(2)}, u32[]{:S(2)}) collective-permute-start(bf16[128,512]{1,0:T(8,128)(2,1)} %copy.58), channel_id=1, source_target_pairs={{0,16},{16,32},{32,48},{48,64},{64,80},{80,96},{96,112},{112,128},... | collective-permute-start | bytes 393224 | tf_op jit(solution)/shard_map/while/body/eval_jaxpr/ppermute | solution.py:17
  487.9 13.8 %collective-permute-start.1 = (bf16[128,64]{1,0:T(8,128)(2,1)}, bf16[128,64]{1,0:T(8,128)(2,1)S(1)}, u32[]{:S(2)}, u32[]{:S(2)}) collective-permute-start(bf16[128,64]{1,0:T(8,128)(2,1)} %copy.59), channel_id=1, source_target_pairs={{0,16},{16,32},{32,48},{48,64},{64,80},{80,96},{96,112},{112,128},... | collective-permute-start | bytes 49160 | tf_op jit(solution)/shard_map/while/body/eval_jaxpr/ppermute | solution.py:17
  502.4 16.0 %collective-permute-start = (bf16[128,512]{1,0:T(8,128)(2,1)}, bf16[128,512]{1,0:T(8,128)(2,1)S(1)}, u32[]{:S(2)}, u32[]{:S(2)}) collective-permute-start(bf16[128,512]{1,0:T(8,128)(2,1)} %copy.58), channel_id=1, source_target_pairs={{0,16},{16,32},{32,48},{48,64},{64,80},{80,96},{96,112},{112,128},... | collective-permute-start | bytes 393224 | tf_op jit(solution)/shard_map/while/body/eval_jaxpr/ppermute | solution.py:17
  519.1 16.0 %collective-permute-start = (bf16[128,512]{1,0:T(8,128)(2,1)}, bf16[128,512]{1,0:T(8,128)(2,1)S(1)}, u32[]{:S(2)}, u32[]{:S(2)}) collective-permute-start(bf16[128,512]{1,0:T(8,128)(2,1)} %copy.58), channel_id=1, source_target_pairs={{0,16},{16,32},{32,48},{48,64},{64,80},{80,96},{96,112},{112,128},... | collective-permute-start | bytes 393224 | tf_op jit(solution)/shard_map/while/body/eval_jaxpr/ppermute | solution.py:17
  (17 other events, 217.1 us)
Sparse Core Ops, SparseCore 0:
  539.4 109.2 reduce-scatter.1
where the time goes:
time: 662 us; the launch traced here: 655 us
  waiting for transfers between devices  282 us (43%)
  starting transfers between devices  126 us (19%)
  local copies, waits for them, and re-layouts  104 us (16%)
  matrix products  85.3 us (13%)
  loops' own time  38.7 us (6%)
  between operations  14.8 us (2%)
    ppermute x62, waiting for transfers between devices, from_behind(): return lax.ppermute(block, axis, route)  173 us
    ppermute x62, starting transfers between devices, from_behind(): return lax.ppermute(block, axis, route)  126 us
    reduce_scatter x1, waiting for transfers between devices, body(): lax.psum_scatter(jnp.dot(head_out, w_out, preferred_element_type=jnp.floa...  109 us
    while x62, local copies, waits for them, and re-layouts  39.4 us
    slice x64, local copies, waits for them, and re-layouts, attend(): active = (begin_at <= query_pos[-1]) & (key_seg[-1] >= query_seg[0])  37.3 us
    another operation x1, loops' own time, body(): lax.fori_loop(0, axis_size - 1, advance, (initial, (latent, rope_keys)))  37 us
    dot_general x22, matrix products, update(): jnp.dot(powers.astype(jnp.bfloat16), lat_block, preferred_element_type=jn...  31.9 us
    dot_general x22, matrix products, update(): scores = jnp.dot(absorbed, lat_block.T, preferred_element_type=jnp.float32)  26.5 us
  transfers between devices with their start and end apart: 63, of which 32 were waited for; matrix products, arithmetic and copies ran while one was open for 25% of the time, Pallas kernels for 0%

commit v1 on v0

v1 whole, which is shorter than its diff:
```python
import functools
import math

import jax
import jax.numpy as jnp
from jax import lax
from jax.experimental import pallas as pl
from jax.experimental.pallas import tpu as pltpu
from jax.sharding import PartitionSpec as P

LAT = 512
NOPE = 128
ROPE = 64
VDIM = 128
WIDE = 640
ROWS = 128
HEADS = 4
OUT = 3584
XBLOCKS = (3, 2)
COLUMNS = ((0, 1024), (1024, 1024), (2048, 1024), (3072, 512))
MESH = pl.DeviceIdType.MESH
NT = (((1,), (1,)), ((), ()))


def device(x, y, z, core):
    x, y, z = lax.rem(x, 4), lax.rem(y, 4), lax.rem(z, 16)
    return (y * 8 + lax.rem(z, 8), x * 4 + lax.div(z, 8) * 2 + core)


def remote(src, dst, send, recv, target):
    return pltpu.make_async_remote_copy(
        src_ref=src, dst_ref=dst, send_sem=send, recv_sem=recv, device_id=target, device_id_type=MESH
    )


def kernel(
    qn_ref, qr_ref, lat_ref, rope_ref, seg_ref, wuk_hbm, wuv_hbm, wout_hbm, o_ref,
    kb, kown, qb, wuk, wuv, wout, acc, m_ref, l_ref, hob, sib_out, sib_in, own, x_out, x_in, total, z_out, z_in,
    w_sem, zs, zr, ys, yr, xs, xr, cs, cr, rcs, rcr, rxs, rxr, rzs, rzr,
):
    ctx, head = lax.axis_index("ctx"), lax.axis_index("head")
    y, zlo = lax.div(ctx, 8), lax.rem(ctx, 8)
    x, zhi, core = lax.div(head, 4), lax.rem(lax.div(head, 2), 2), lax.rem(head, 2)
    z = zhi * 8 + zlo
    other = 1 - core
    sibling = device(x, y, z, other)

    loads = [
        pltpu.make_async_copy(a, b, w_sem.at[i])
        for i, (a, b) in enumerate(((wuk_hbm, wuk), (wuv_hbm, wuv), (wout_hbm, wout)))
    ]
    for load in loads:
        load.start()

    barrier = pltpu.get_barrier_semaphore()
    partners = [device(x, y, z + s, core) for s in (1, 2, 3, 4, 15, 14, 13, 12, 8)]
    partners += [device(x, y + s, z, core) for s in (1, 2, 3)]
    partners += [device(x + s, y, z, core) for s in (1, 2, 3)]
    partners += [sibling]
    for partner in partners:
        pl.semaphore_signal(barrier, inc=1, device_id=partner, device_id_type=MESH)

    keys = jnp.concatenate([lat_ref[...], rope_ref[...], jnp.zeros((ROWS, WIDE - LAT - ROPE), jnp.bfloat16)], axis=1)
    kown[...] = keys.reshape(8, 16, WIDE)

    def by_x(block_z):
        return lax.rem(block_z, 4) < jnp.where(block_z < 4, XBLOCKS[0], XBLOCKS[1])

    @pl.when(by_x(zlo))
    def _():
        kb[ctx, 4 * core + x] = kown[4 * core + x]

    @pl.when(jnp.logical_not(by_x(zlo)))
    def _():
        kb[ctx, pl.ds(4 * core, 4)] = kown[pl.ds(4 * core, 4)]

    pl.semaphore_wait(barrier, len(partners))

    steps = [1, 15, 2, 14, 3, 13, 4 + 8 * core]

    def z_copies(i, block):
        target = device(x, y, z + steps[i], core)
        narrow = kb.at[block, 4 * core + x]
        wide = kb.at[block, pl.ds(4 * core, 4)]
        return (
            remote(narrow, narrow, zs.at[i], zr.at[i], target),
            remote(wide, wide, zs.at[i], zr.at[i], target),
        )

    def z_each(i, block_z, act):
        narrow, wide = z_copies(i, y * 8 + block_z)

        @pl.when(by_x(block_z))
        def _():
            act(narrow)

        @pl.when(jnp.logical_not(by_x(block_z)))
        def _():
            act(wide)

    for i in range(7):
        z_each(i, zlo, lambda copy: copy.start())

    loads[0].wait()
    for h in range(HEADS):
        absorbed = lax.dot_general(
            qn_ref[:, h * NOPE:(h + 1) * NOPE], wuk[:, h * NOPE:(h + 1) * NOPE], NT, preferred_element_type=jnp.float32
        ).astype(jnp.bfloat16)
        tail = jnp.concatenate(
            [qr_ref[:, h * ROPE:(h + 1) * ROPE], jnp.zeros((ROWS, WIDE - LAT - ROPE), jnp.bfloat16)], axis=1
        )
        qb[h * ROWS:(h + 1) * ROWS, :LAT] = absorbed
        qb[h * ROWS:(h + 1) * ROWS, LAT:] = tail

    seg = seg_ref[...]
    own_seg = seg_ref[pl.ds(ctx, 1), :]
    first = jnp.zeros((1, ROWS), jnp.float32)
    for e in range(7):
        count = jnp.sum(jnp.where(seg == e, 1.0, 0.0), axis=1, keepdims=True)
        count = jnp.sum(count, axis=0, keepdims=True)
        first = first + jnp.where(own_seg > e, count, 0.0)
    down = lax.broadcasted_iota(jnp.int32, (ROWS, ROWS), 0)
    across = lax.broadcasted_iota(jnp.int32, (ROWS, ROWS), 1)
    first = jnp.sum(jnp.where(down == across, first, 0.0), axis=1, keepdims=True).astype(jnp.int32)
    first2 = jnp.concatenate([first, first], axis=0)
    factor = math.log2(math.e) / math.sqrt(NOPE + ROPE)

    diagonal = (across <= down) & (across + ctx * ROWS >= first)
    for h in range(HEADS):
        rows = slice(h * ROWS, (h + 1) * ROWS)
        scores = lax.dot_general(qb[rows, :], keys, NT, preferred_element_type=jnp.float32) * factor
        scores = jnp.where(diagonal, scores, -jnp.inf)
        top = jnp.broadcast_to(jnp.max(scores, axis=1, keepdims=True), (ROWS, 128))
        powers = jnp.exp2(scores - top)
        m_ref[rows, :] = top
        l_ref[rows, :] = powers
        acc[rows, :] = jnp.dot(powers.astype(jnp.bfloat16), keys[:, :LAT], preferred_element_type=jnp.float32)

    for i in range(7):
        z_each(i, lax.rem(zlo + 16 - steps[i], 8), lambda copy: copy.wait_recv())

    def y_copies(row, g, hop, target):
        begin = row * 8 + 4 * g
        narrow = kb.at[pl.ds(begin, XBLOCKS[g]), 4 * core + x]
        wide = kb.at[pl.ds(begin + XBLOCKS[g], 4 - XBLOCKS[g]), pl.ds(4 * core, 4)]
        return [
            remote(part, part, ys.at[hop - 1, g, i], yr.at[hop - 1, g, i], target)
            for i, part in enumerate((narrow, wide))
        ]

    def y_each(act):
        for g in range(2):
            for hop in (1, 2, 3):
                wanted = y + hop <= 3
                if hop == 3:
                    wanted = wanted & (zlo <= 4 * g + 3)

                @pl.when(wanted)
                def _():
                    for copy in y_copies(y, g, hop, device(x, y + hop, z, core)):
                        act(copy)

    y_each(lambda copy: copy.start())

    def needed(k, g):
        return (y >= k) & ((k > 0) | (zlo > 4 * g)) & ((k < 3) | (zlo <= 4 * g + 3))

    def x_copies(k, g):
        begin = (y - k) * 8 + 4 * g
        copies = []
        for s in (1, 2, 3):
            piece = kb.at[pl.ds(begin, XBLOCKS[g]), 4 * core + x]
            copies.append(remote(piece, piece, xs.at[k, g, s - 1], xr.at[k, g, s - 1], device(x + s, y, z, core)))
        return copies

    def core_copy(k, g):
        begin = (y - k) * 8 + 4 * g
        piece = kb.at[pl.ds(begin, 4), pl.ds(4 * core, 4)]
        return remote(piece, piece, cs.at[k, g], cr.at[k, g], sibling)

    def stage_x(k, g, from_y):
        @pl.when(needed(k, g))
        def _():
            if from_y:
                for copy in y_copies(y - k, g, k, sibling):
                    copy.wait_recv()
            for copy in x_copies(k, g):
                copy.start()

    def stage_core(k, g):
        @pl.when(needed(k, g))
        def _():
            for copy in x_copies(k, g):
                copy.wait_recv()
            core_copy(k, g).start()

    def stage_attend(k, g):
        @pl.when(needed(k, g))
        def _():
            core_copy(k, g).wait_recv()
            begin = (y - k) * 8 + 4 * g
            block = kb[pl.ds(begin, 4)].reshape(512, WIDE)
            place = begin * ROWS + lax.broadcasted_iota(jnp.int32, (256, 512), 1)
            visible = (place >= first2) & (place < ctx * ROWS)
            for half in range(2):
                rows = slice(half * 256, (half + 1) * 256)
                scores = lax.dot_general(qb[rows, :], block, NT, preferred_element_type=jnp.float32) * factor
                scores = jnp.where(visible, scores, -jnp.inf)
                before = m_ref[rows, :]
                top = jnp.maximum(before, jnp.max(scores, axis=1, keepdims=True))
                shrink = jnp.exp2(before - top)
                powers = jnp.exp2(scores - jnp.concatenate([top] * 4, axis=1))
                m_ref[rows, :] = top
                l_ref[rows, :] = l_ref[rows, :] * shrink + (
                    (powers[:, :128] + powers[:, 128:256]) + (powers[:, 256:384] + powers[:, 384:])
                )
                acc[rows, :] = acc[rows, :] * jnp.concatenate([shrink] * 4, axis=1) + jnp.dot(
                    powers.astype(jnp.bfloat16), block[:, :LAT], preferred_element_type=jnp.float32
                )

    stage_x(0, 0, False)
    stage_x(0, 1, False)
    stage_core(0, 0)

    def step(k, carry):
        @pl.when(k < 3)
        def _():
            stage_x(k + 1, 0, True)

        stage_core(k, 1)
        stage_attend(k, 0)

        @pl.when(k < 3)
        def _():
            stage_x(k + 1, 1, True)
            stage_core(k + 1, 0)

        stage_attend(k, 1)
        return carry

    lax.fori_loop(0, 4, step, 0)

    loads[1].wait()
    parts = []
    for h in range(HEADS):
        rows = slice(h * ROWS, (h + 1) * ROWS)
        sums = jnp.sum(l_ref[rows, :], axis=1, keepdims=True)
        context = (acc[rows, :] / sums).astype(jnp.bfloat16)
        parts.append(jnp.dot(context, wuv[:, h * VDIM:(h + 1) * VDIM], preferred_element_type=jnp.float32))
    head_out = jnp.concatenate(parts, axis=1)
    order = [32 * i + 16 * j + 8 * c for c in range(2) for i in range(4) for j in range(2)]
    hob[...] = jnp.concatenate([head_out[r:r + 8] for r in order], axis=0).astype(jnp.bfloat16)
    loads[2].wait()

    def rc_copy(j):
        begin, width = COLUMNS[j]
        return remote(
            sib_out.at[:, pl.ds(begin, width)], sib_in.at[:, pl.ds(begin, width)], rcs.at[j], rcr.at[j], sibling
        )

    def rx_copies(j):
        begin, width = COLUMNS[j]
        copies = []
        for s in (1, 2, 3):
            to = lax.rem(x + s, 4)
            copies.append(
                remote(
                    x_out.at[pl.ds(pl.multiple_of(16 * to, 16), 16), pl.ds(begin, width)],
                    x_in.at[s - 1, :, pl.ds(begin, width)],
                    rxs.at[j, s - 1],
                    rxr.at[j, s - 1],
                    device(x + s, y, z, core),
                )
            )
        return copies

    def rz_copy(j):
        begin, width = COLUMNS[j][0] // 2, COLUMNS[j][1] // 2
        return remote(
            z_out.at[:, pl.ds(begin, width)], z_in.at[:, pl.ds(begin, width)], rzs.at[j], rzr.at[j],
            device(x, y, z + 8, core),
        )

    theirs = hob[pl.ds(pl.multiple_of(64 * other, 64), 64), :]
    mine = hob[pl.ds(pl.multiple_of(64 * core, 64), 64), :]
    for j, (begin, width) in enumerate(COLUMNS):
        sib_out[:, begin:begin + width] = jnp.dot(
            theirs, wout[:, begin:begin + width], preferred_element_type=jnp.float32
        ).astype(jnp.bfloat16)
        rc_copy(j).start()
    for j, (begin, width) in enumerate(COLUMNS):
        columns = slice(begin, begin + width)
        part = jnp.dot(mine, wout[:, columns], preferred_element_type=jnp.float32)
        rc_copy(j).wait_recv()
        part = part + sib_in[:, columns].astype(jnp.float32)
        own[:, columns] = part
        x_out[:, columns] = part.astype(jnp.bfloat16)
        for copy in rx_copies(j):
            copy.start()
    for j, (begin, width) in enumerate(COLUMNS):
        columns = slice(begin, begin + width)
        for copy in rx_copies(j):
            copy.wait_recv()
        part = own[pl.ds(pl.multiple_of(16 * x, 16), 16), columns]
        for s in range(3):
            part = part + x_in[s, :, columns].astype(jnp.float32)
        total[:, columns] = part
        away = total[pl.ds(pl.multiple_of(8 - 8 * zhi, 8), 8), columns]
        half = width // 2
        z_out[:, begin // 2:begin // 2 + half] = jnp.concatenate([away[:, :half], away[:, half:]], axis=0).astype(
            jnp.bfloat16
        )
        rz_copy(j).start()
    for j, (begin, width) in enumerate(COLUMNS):
        columns = slice(begin, begin + width)
        half = width // 2
        rz_copy(j).wait_recv()
        came = z_in[:, begin // 2:begin // 2 + half].astype(jnp.float32)
        came = jnp.concatenate([came[:8], came[8:]], axis=1)
        o_ref[:, columns] = (total[pl.ds(pl.multiple_of(8 * zhi, 8), 8), columns] + came).astype(jnp.bfloat16)

    for i in range(7):
        z_each(i, zlo, lambda copy: copy.wait_send())
    y_each(lambda copy: copy.wait_send())

    def drain(k, carry):
        for g in range(2):
            @pl.when(needed(k, g))
            def _():
                for copy in x_copies(k, g):
                    copy.wait_send()
                core_copy(k, g).wait_send()

        return carry

    lax.fori_loop(0, 4, drain, 0)
    for j in range(len(COLUMNS)):
        rc_copy(j).wait_send()
        for copy in rx_copies(j):
            copy.wait_send()
        rz_copy(j).wait_send()


def body(q_nope, q_rope, latent, rope_keys, seg_ids, w_uk, w_uv, w_out):
    vmem = pl.BlockSpec(memory_space=pltpu.VMEM)
    hbm = pl.BlockSpec(memory_space=pl.ANY)
    bf16, f32 = jnp.bfloat16, jnp.float32
    dma, chunks = pltpu.SemaphoreType.DMA, len(COLUMNS)
    return pl.pallas_call(
        kernel,
        out_shape=jax.ShapeDtypeStruct((8, OUT), bf16),
        in_specs=[vmem] * 5 + [hbm] * 3,
        out_specs=vmem,
        scratch_shapes=[
            pltpu.VMEM((32, 8, 16, WIDE), bf16),
            pltpu.VMEM((8, 16, WIDE), bf16),
            pltpu.VMEM((HEADS * ROWS, WIDE), bf16),
            pltpu.VMEM((LAT, HEADS * NOPE), bf16),
            pltpu.VMEM((LAT, HEADS * VDIM), bf16),
            pltpu.VMEM((HEADS * VDIM, OUT), bf16),
            pltpu.VMEM((HEADS * ROWS, LAT), f32),
            pltpu.VMEM((HEADS * ROWS, 128), f32),
            pltpu.VMEM((HEADS * ROWS, 128), f32),
            pltpu.VMEM((ROWS, HEADS * VDIM), bf16),
            pltpu.VMEM((64, OUT), bf16),
            pltpu.VMEM((64, OUT), bf16),
            pltpu.VMEM((64, OUT), f32),
            pltpu.VMEM((64, OUT), bf16),
            pltpu.VMEM((3, 16, OUT), bf16),
            pltpu.VMEM((16, OUT), f32),
            pltpu.VMEM((16, OUT // 2), bf16),
            pltpu.VMEM((16, OUT // 2), bf16),
            dma((3,)),
            dma((7,)), dma((7,)),
            dma((3, 2, 2)), dma((3, 2, 2)),
            dma((4, 2, 3)), dma((4, 2, 3)),
            dma((4, 2)), dma((4, 2)),
            dma((chunks,)), dma((chunks,)),
            dma((chunks, 3)), dma((chunks, 3)),
            dma((chunks,)), dma((chunks,)),
        ],
        compiler_params=pltpu.CompilerParams(
            collective_id=0, has_side_effects=True, vmem_limit_bytes=48 * 2**20
        ),
    )(q_nope, q_rope, latent, rope_keys, seg_ids.reshape(32, 128), w_uk, w_uv, w_out)


def solution(mesh):
    placed = (
        P("ctx", "head"),
        P("ctx", "head"),
        P("ctx", None),
        P("ctx", None),
        P(),
        P(None, "head"),
        P(None, "head"),
        P("head", None),
    )
    return jax.shard_map(
        body, mesh=mesh, in_specs=placed, out_specs=P(("ctx", "head"), None), check_vma=False
    )
```

time: 662 us -> 82.7 us (0.12)
  the two profiles are of different devices: /device:TPU:24 before, /device:TPU:80 now
where the time goes in v1:
time: 82.7 us; the launch traced here: 82.2 us
  Pallas kernels  73.3 us (89%)
  local copies, waits for them, and re-layouts  8.94 us (11%)
    pallas_call x1, Pallas kernels, body(): pl.pallas_call(kernel, out_shape=jax.ShapeDtypeStruct((8, OUT), bf16), in...  73.3 us
    unnamed x16, local copies, waits for them, and re-layouts  8.94 us

profile of v1, /device:TPU:80, one launch (start us, length us, event | category | flops | bytes accessed | tf_op | source)
XLA Modules:
  0.0 82.2 jit_solution(5520704043663578194)
XLA Ops:
  0.0 0.8 %copy.9.rope_ref = bf16[128,64]{1,0:T(8,128)(2,1)S(1)} copy(bf16[128,64]{0,1:T(8,128)(2,1)} %param.11) | data formatting | bytes 32768 | tf_op args[3]
  0.8 0.0 copy-start
  0.8 2.0 %copy-done = bf16[512,3584]{1,0:T(8,128)(2,1)S(1)} copy-done((bf16[512,3584]{1,0:T(8,128)(2,1)S(1)}, bf16[512,3584]{1,0:T(8,128)(2,1)}, u32[]{:S(2)}) %copy-start) | copy-done | bytes 3670040
  2.9 0.0 copy-start.1
  2.9 1.0 %copy-done.1 = bf16[512,512]{1,0:T(8,128)(2,1)S(1)} copy-done((bf16[512,512]{1,0:T(8,128)(2,1)S(1)}, bf16[512,512]{1,0:T(8,128)(2,1)}, u32[]{:S(2)}) %copy-start.1) | copy-done | bytes 524312
  3.9 0.0 copy-start.2
  3.9 1.0 %copy-done.2 = bf16[512,512]{1,0:T(8,128)(2,1)S(1)} copy-done((bf16[512,512]{1,0:T(8,128)(2,1)S(1)}, bf16[512,512]{1,0:T(8,128)(2,1)}, u32[]{:S(2)}) %copy-start.2) | copy-done | bytes 524312
  5.0 0.0 copy-start.3
  5.0 0.9 %copy-done.3 = bf16[128,512]{1,0:T(8,128)(2,1)S(1)} copy-done((bf16[128,512]{1,0:T(8,128)(2,1)S(1)}, bf16[128,512]{1,0:T(8,128)(2,1)}, u32[]{:S(2)}) %copy-start.3) | copy-done | bytes 131096
  5.9 0.0 copy-start.4
  5.9 0.9 %copy-done.4 = bf16[128,512]{1,0:T(8,128)(2,1)S(1)} copy-done((bf16[128,512]{1,0:T(8,128)(2,1)S(1)}, bf16[128,512]{1,0:T(8,128)(2,1)}, u32[]{:S(2)}) %copy-start.4) | copy-done | bytes 131096
  6.8 0.0 copy-start.5
  6.8 0.8 %copy-done.5 = bf16[128,256]{1,0:T(8,128)(2,1)S(1)} copy-done((bf16[128,256]{1,0:T(8,128)(2,1)S(1)}, bf16[128,256]{1,0:T(8,128)(2,1)}, u32[]{:S(2)}) %copy-start.5) | copy-done | bytes 65560
  7.6 0.0 copy-start.6
  7.6 0.7 copy-done.6
  8.3 73.3 %shard_map.82 = bf16[8,3584]{1,0:T(8,128)(2,1)S(1)} custom-call(bf16[128,512]{1,0:T(8,128)(2,1)S(1)} %copy-done.3, bf16[128,256]{1,0:T(8,128)(2,1)S(1)} %copy-done.5, bf16[128,512]{1,0:T(8,128)(2,1)S(1)} %copy-done.4, bf16[128,64]{1,0:T(8,128)(2,1)S(1)} %copy.9.rope_ref, s32[32,128]{1,0:T(8,128)S(1)} %bitcast.1, bf16[512,512]{1,0:T(8,128)(2,1)S(1)} %copy-done.1, ...), custom_call_target="tpu_custom_call" | custom-call | tf_op jit(solution)/shard_map/pallas_call | solution.py:349
  81.6 0.6 copy.11
Async XLA Ops:
  0.8 2.0 %copy-start = (bf16[512,3584]{1,0:T(8,128)(2,1)S(1)}, bf16[512,3584]{1,0:T(8,128)(2,1)}, u32[]{:S(2)}) copy-start(bf16[512,3584]{1,0:T(8,128)(2,1)} %wout_hbm.1) | copy-start | bytes 11010052
  2.9 1.0 %copy-start.1 = (bf16[512,512]{1,0:T(8,128)(2,1)S(1)}, bf16[512,512]{1,0:T(8,128)(2,1)}, u32[]{:S(2)}) copy-start(bf16[512,512]{1,0:T(8,128)(2,1)} %wuk_hbm.1) | copy-start | bytes 1572868
  3.9 1.0 %copy-start.2 = (bf16[512,512]{1,0:T(8,128)(2,1)S(1)}, bf16[512,512]{1,0:T(8,128)(2,1)}, u32[]{:S(2)}) copy-start(bf16[512,512]{1,0:T(8,128)(2,1)} %wuv_hbm.1) | copy-start | bytes 1572868
  5.0 0.9 %copy-start.3 = (bf16[128,512]{1,0:T(8,128)(2,1)S(1)}, bf16[128,512]{1,0:T(8,128)(2,1)}, u32[]{:S(2)}) copy-start(bf16[128,512]{1,0:T(8,128)(2,1)} %qn_ref.1) | copy-start | bytes 393220
  5.9 0.9 %copy-start.4 = (bf16[128,512]{1,0:T(8,128)(2,1)S(1)}, bf16[128,512]{1,0:T(8,128)(2,1)}, u32[]{:S(2)}) copy-start(bf16[128,512]{1,0:T(8,128)(2,1)} %lat_ref.1) | copy-start | bytes 393220
  6.8 0.8 %copy-start.5 = (bf16[128,256]{1,0:T(8,128)(2,1)S(1)}, bf16[128,256]{1,0:T(8,128)(2,1)}, u32[]{:S(2)}) copy-start(bf16[128,256]{1,0:T(8,128)(2,1)} %qr_ref.1) | copy-start | bytes 196612
  7.6 0.7 copy-start.6

commit v2 on v1

v2 whole, which is shorter than its diff:
```python
import functools
import math

import jax
import jax.numpy as jnp
from jax import lax
from jax.experimental import pallas as pl
from jax.experimental.pallas import tpu as pltpu
from jax.sharding import PartitionSpec as P

LAT = 512
NOPE = 128
ROPE = 64
VDIM = 128
WIDE = 640
ROWS = 128
HEADS = 4
OUT = 3584
GROUPS = 6
COLUMNS = ((0, 1024), (1024, 1024), (2048, 1024), (3072, 512))
VMEM_BYTES = 62 * 2**20
MESH = pl.DeviceIdType.MESH
NT = (((1,), (1,)), ((), ()))


def device(x, y, z, core):
    x, y, z = lax.rem(x, 4), lax.rem(y, 4), lax.rem(z, 16)
    return (y * 8 + lax.rem(z, 8), x * 4 + lax.div(z, 8) * 2 + core)


def remote(src, dst, send, recv, target):
    return pltpu.make_async_remote_copy(
        src_ref=src, dst_ref=dst, send_sem=send, recv_sem=recv, device_id=target, device_id_type=MESH
    )


def kernel(
    qn_hbm, qr_hbm, lat_hbm, rope_hbm, seg_hbm, wuk_hbm, wuv_hbm, wout_hbm, o_ref,
    qn_ref, qr_ref, lat_ref, rope_ref, seg_ref, wuk, wuv, wout,
    kb, kown, qb, acc, m_ref, l_ref, hob, sib_out, sib_in, own, x_out, x_in, total, z_out, z_in,
    w_sem, zs, zr, ys, yr, ws, wr, xs, xr, rs, rr, cs, cr, rcs, rcr, rxs, rxr, rzs, rzr,
):
    ctx, head = lax.axis_index("ctx"), lax.axis_index("head")
    y, zlo = lax.div(ctx, 8), lax.rem(ctx, 8)
    x, zhi, core = lax.div(head, 4), lax.rem(lax.div(head, 2), 2), lax.rem(head, 2)
    z = zhi * 8 + zlo
    last_row = y == 3
    other = 1 - core
    sibling = device(x, y, z, other)
    quarter = 4 * core + x

    barrier = pltpu.get_barrier_semaphore()
    partners = [device(x, y, z + s, core) for s in (1, 2, 3, 4, 15, 14, 13, 12, 8)]
    partners += [device(x, y + s, z, core) for s in (1, 2, 3)]
    partners += [device(x + s, y, z, core) for s in (1, 2, 3)]
    partners += [sibling]
    for partner in partners:
        pl.semaphore_signal(barrier, inc=1, device_id=partner, device_id_type=MESH)

    pairs = (
        (lat_hbm, lat_ref), (rope_hbm, rope_ref), (wuk_hbm, wuk), (qn_hbm, qn_ref), (qr_hbm, qr_ref),
        (seg_hbm, seg_ref), (wuv_hbm, wuv), (wout_hbm, wout),
    )
    loads = [pltpu.make_async_copy(a, b, w_sem.at[i]) for i, (a, b) in enumerate(pairs)]
    for load in loads:
        load.start()

    loads[0].wait()
    loads[1].wait()
    rope = jnp.transpose(rope_ref[...].astype(jnp.float32)).astype(jnp.bfloat16)
    kown[...] = jnp.concatenate(
        [lat_ref[...], rope, jnp.zeros((ROWS, WIDE - LAT - ROPE), jnp.bfloat16)], axis=1
    ).reshape(8, 16, WIDE)

    @pl.when(jnp.logical_not(last_row))
    def _():
        kb[ctx, quarter] = kown[quarter]

    pl.semaphore_wait(barrier, len(partners))

    steps = [1, 15, 2, 14, 3, 13, 4 + 8 * core]

    def z_send(i):
        wanted = jnp.logical_not(last_row) | (lax.rem(zlo + steps[i], 8) > zlo)
        return wanted, remote(
            kown.at[quarter], kb.at[ctx, quarter], zs.at[i], zr.at[i], device(x, y, z + steps[i], core)
        )

    def z_recv(i):
        source = lax.rem(zlo + 16 - steps[i], 8)
        piece = kb.at[y * 8 + source, quarter]
        return source, remote(piece, piece, zs.at[i], zr.at[i], sibling)

    def y_one(block_z):
        piece = kb.at[y * 8 + block_z, quarter]
        g = lax.div(block_z, 4)
        return remote(piece, piece, ys.at[0, g], yr.at[0, g], device(x, y + 1, z, core))

    def y_three(block_z):
        return remote(
            kb.at[block_z, quarter], kb.at[24 + block_z, quarter], ws.at[block_z], wr.at[block_z],
            device(x, 3, z, core),
        )

    def y_group(hop, g, row):
        piece = kb.at[pl.ds(row * 8 + 4 * g, 4), quarter]
        return remote(piece, piece, ys.at[hop - 1, g], yr.at[hop - 1, g], device(x, y + hop, z, core))

    onward, back = jnp.where(core == 0, 1, 3), jnp.where(core == 0, 3, 1)
    sides = (onward, back)

    def place_of(i):
        k, g = lax.div(i, 2), lax.rem(i, 2)
        return (y - k) * 8 + 4 * g

    def needed(i):
        k, g = lax.div(i, 2), lax.rem(i, 2)
        return (y >= k) & ((k > 0) | last_row | (zlo > 4 * g))

    def x_one(block_z, side):
        piece = kb.at[y * 8 + block_z, quarter]
        g = lax.div(block_z, 4)
        return remote(piece, piece, xs.at[g, side], xr.at[g, side], device(x + sides[side], y, z, core))

    def x_group(i, side):
        piece = kb.at[pl.ds(place_of(i), 4), quarter]
        return remote(piece, piece, xs.at[i, side], xr.at[i, side], device(x + sides[side], y, z, core))

    def x_pass(i):
        piece = kb.at[pl.ds(place_of(i), 4), 4 * core + lax.rem(x + back, 4)]
        return remote(piece, piece, rs.at[i], rr.at[i], device(x + onward, y, z, core))

    def core_copy(i):
        piece = kb.at[pl.ds(place_of(i), 4), pl.ds(4 * core, 4)]
        return remote(piece, piece, cs.at[i], cr.at[i], sibling)

    def x_start(block_z):
        @pl.when(last_row | (zlo > 4 * lax.div(block_z, 4)))
        def _():
            x_one(block_z, 0).start()
            x_one(block_z, 1).start()

    def forward(block_z):
        @pl.when(jnp.logical_not(last_row))
        def _():
            y_one(block_z).start()

        @pl.when((y == 0) & (block_z >= zlo))
        def _():
            y_three(block_z).start()

    for i in range(7):
        wanted, copy = z_send(i)
        pl.when(wanted)(copy.start)
    forward(zlo)

    for load in loads[2:5]:
        load.wait()
    for h in range(HEADS):
        absorbed = lax.dot_general(
            qn_ref[:, h * NOPE:(h + 1) * NOPE], wuk[:, h * NOPE:(h + 1) * NOPE], NT, preferred_element_type=jnp.float32
        ).astype(jnp.bfloat16)
        tail = jnp.concatenate(
            [qr_ref[:, h * ROPE:(h + 1) * ROPE], jnp.zeros((ROWS, WIDE - LAT - ROPE), jnp.bfloat16)], axis=1
        )
        qb[h * ROWS:(h + 1) * ROWS, :LAT] = absorbed
        qb[h * ROWS:(h + 1) * ROWS, LAT:] = tail

    @pl.when(last_row)
    def _():
        y_three(zlo).wait_recv()

    x_start(zlo)
    for i in range(7):
        source, copy = z_recv(i)

        @pl.when(jnp.logical_not(last_row) | (source < zlo))
        def _():
            copy.wait_recv()

        @pl.when(last_row & (source > zlo))
        def _():
            y_three(source).wait_recv()

        forward(source)
        x_start(source)

    for g in range(2):
        @pl.when(y < 2)
        def _():
            y_group(2, g, y).start()

    loads[5].wait()
    seg = seg_ref[...]
    own_seg = seg_ref[pl.ds(ctx, 1), :]
    first = jnp.zeros((1, ROWS), jnp.float32)
    for e in range(7):
        count = jnp.sum(jnp.where(seg == e, 1.0, 0.0), axis=1, keepdims=True)
        count = jnp.sum(count, axis=0, keepdims=True)
        first = first + jnp.where(own_seg > e, count, 0.0)
    down = lax.broadcasted_iota(jnp.int32, (ROWS, ROWS), 0)
    across = lax.broadcasted_iota(jnp.int32, (ROWS, ROWS), 1)
    first = jnp.sum(jnp.where(down == across, first, 0.0), axis=1, keepdims=True).astype(jnp.int32)
    first2 = jnp.concatenate([first, first], axis=0)
    factor = math.log2(math.e) / math.sqrt(NOPE + ROPE)

    keys = kown[...].reshape(ROWS, WIDE)
    diagonal = (across <= down) & (across + ctx * ROWS >= first)
    for h in range(HEADS):
        rows = slice(h * ROWS, (h + 1) * ROWS)
        scores = lax.dot_general(qb[rows, :], keys, NT, preferred_element_type=jnp.float32) * factor
        scores = jnp.where(diagonal, scores, -jnp.inf)
        top = jnp.broadcast_to(jnp.max(scores, axis=1, keepdims=True), (ROWS, 128))
        powers = jnp.exp2(scores - top)
        m_ref[rows, :] = top
        l_ref[rows, :] = powers
        acc[rows, :] = jnp.dot(powers.astype(jnp.bfloat16), keys[:, :LAT], preferred_element_type=jnp.float32)

    def stage_x(i):
        k, g = lax.div(i, 2), lax.rem(i, 2)

        @pl.when((i < GROUPS) & needed(i))
        def _():
            y_group(k, g, y - k).wait_recv()
            x_group(i, 0).start()
            x_group(i, 1).start()

    def stage_pass(i):
        @pl.when((i < GROUPS) & needed(i))
        def _():
            x_group(i, 0).wait_recv()
            x_pass(i).start()

    def stage_core(i):
        @pl.when((i >= 0) & (i < GROUPS) & needed(i))
        def _():
            x_group(i, 1).wait_recv()
            x_pass(i).wait_recv()
            core_copy(i).start()

    def stage_attend(i):
        @pl.when((i >= 0) & needed(i))
        def _():
            core_copy(i).wait_recv()
            begin = place_of(i)
            block = kb[pl.ds(begin, 4)].reshape(512, WIDE)
            place = begin * ROWS + lax.broadcasted_iota(jnp.int32, (256, 512), 1)
            place = jnp.where(last_row & (place >= ctx * ROWS), place - 24 * ROWS, place)
            visible = (place >= first2) & (place < ctx * ROWS)
            for half in range(2):
                rows = slice(half * 256, (half + 1) * 256)
                scores = lax.dot_general(qb[rows, :], block, NT, preferred_element_type=jnp.float32) * factor
                scores = jnp.where(visible, scores, -jnp.inf)
                before = m_ref[rows, :]
                top = jnp.maximum(before, jnp.max(scores, axis=1, keepdims=True))
                shrink = jnp.exp2(before - top)
                powers = jnp.exp2(scores - jnp.concatenate([top] * 4, axis=1))
                m_ref[rows, :] = top
                l_ref[rows, :] = l_ref[rows, :] * shrink + (
                    (powers[:, :128] + powers[:, 128:256]) + (powers[:, 256:384] + powers[:, 384:])
                )
                acc[rows, :] = acc[rows, :] * jnp.concatenate([shrink] * 4, axis=1) + jnp.dot(
                    powers.astype(jnp.bfloat16), block[:, :LAT], preferred_element_type=jnp.float32
                )

    def step(t, carry):
        stage_x(t + 2)
        stage_pass(t)
        stage_core(t - 1)
        stage_attend(t - 2)
        return carry

    lax.fori_loop(0, GROUPS + 2, step, 0)

    loads[6].wait()
    parts = []
    for h in range(HEADS):
        rows = slice(h * ROWS, (h + 1) * ROWS)
        sums = jnp.sum(l_ref[rows, :], axis=1, keepdims=True)
        context = (acc[rows, :] / sums).astype(jnp.bfloat16)
        parts.append(jnp.dot(context, wuv[:, h * VDIM:(h + 1) * VDIM], preferred_element_type=jnp.float32))
    head_out = jnp.concatenate(parts, axis=1)
    order = [32 * i + 16 * j + 8 * c for c in range(2) for i in range(4) for j in range(2)]
    hob[...] = jnp.concatenate([head_out[r:r + 8] for r in order], axis=0).astype(jnp.bfloat16)
    loads[7].wait()

    def rc_copy(j):
        begin, width = COLUMNS[j]
        return remote(
            sib_out.at[:, pl.ds(begin, width)], sib_in.at[:, pl.ds(begin, width)], rcs.at[j], rcr.at[j], sibling
        )

    def rx_copies(j):
        begin, width = COLUMNS[j]
        copies = []
        for s in (1, 2, 3):
            to = lax.rem(x + s, 4)
            copies.append(
                remote(
                    x_out.at[pl.ds(pl.multiple_of(16 * to, 16), 16), pl.ds(begin, width)],
                    x_in.at[s - 1, :, pl.ds(begin, width)],
                    rxs.at[j, s - 1],
                    rxr.at[j, s - 1],
                    device(x + s, y, z, core),
                )
            )
        return copies

    def rz_copy(j):
        begin, width = COLUMNS[j][0] // 2, COLUMNS[j][1] // 2
        return remote(
            z_out.at[:, pl.ds(begin, width)], z_in.at[:, pl.ds(begin, width)], rzs.at[j], rzr.at[j],
            device(x, y, z + 8, core),
        )

    theirs = hob[pl.ds(pl.multiple_of(64 * other, 64), 64), :]
    mine = hob[pl.ds(pl.multiple_of(64 * core, 64), 64), :]
    swapped = jnp.concatenate([theirs, mine], axis=0)
    for j, (begin, width) in enumerate(COLUMNS):
        columns = slice(begin, begin + width)
        part = jnp.dot(swapped, wout[:, columns], preferred_element_type=jnp.float32)
        sib_out[:, columns] = part[:64].astype(jnp.bfloat16)
        rc_copy(j).start()
        own[:, columns] = part[64:]
    for j, (begin, width) in enumerate(COLUMNS):
        columns = slice(begin, begin + width)
        rc_copy(j).wait_recv()
        part = own[:, columns] + sib_in[:, columns].astype(jnp.float32)
        own[:, columns] = part
        x_out[:, columns] = part.astype(jnp.bfloat16)
        for copy in rx_copies(j):
            copy.start()
    for j, (begin, width) in enumerate(COLUMNS):
        columns = slice(begin, begin + width)
        for copy in rx_copies(j):
            copy.wait_recv()
        part = own[pl.ds(pl.multiple_of(16 * x, 16), 16), columns]
        for s in range(3):
            part = part + x_in[s, :, columns].astype(jnp.float32)
        total[:, columns] = part
        away = total[pl.ds(pl.multiple_of(8 - 8 * zhi, 8), 8), columns]
        half = width // 2
        z_out[:, begin // 2:begin // 2 + half] = jnp.concatenate([away[:, :half], away[:, half:]], axis=0).astype(
            jnp.bfloat16
        )
        rz_copy(j).start()
    for j, (begin, width) in enumerate(COLUMNS):
        columns = slice(begin, begin + width)
        half = width // 2
        rz_copy(j).wait_recv()
        came = z_in[:, begin // 2:begin // 2 + half].astype(jnp.float32)
        came = jnp.concatenate([came[:8], came[8:]], axis=1)
        o_ref[:, columns] = (total[pl.ds(pl.multiple_of(8 * zhi, 8), 8), columns] + came).astype(jnp.bfloat16)

    for i in range(7):
        wanted, copy = z_send(i)
        pl.when(wanted)(copy.wait_send)
    for block_z in range(8):
        @pl.when((y == 0) & (block_z >= zlo))
        def _():
            y_three(block_z).wait_send()
    for g in range(2):
        @pl.when(jnp.logical_not(last_row))
        def _():
            y_group(1, g, y).wait_send()

        @pl.when(y < 2)
        def _():
            y_group(2, g, y).wait_send()

    def drain(i, carry):
        @pl.when(needed(i))
        def _():
            x_group(i, 0).wait_send()
            x_group(i, 1).wait_send()
            x_pass(i).wait_send()
            core_copy(i).wait_send()

        return carry

    lax.fori_loop(0, GROUPS, drain, 0)
    for j in range(len(COLUMNS)):
        rc_copy(j).wait_send()
        for copy in rx_copies(j):
            copy.wait_send()
        rz_copy(j).wait_send()


def body(q_nope, q_rope, latent, rope_keys, seg_ids, w_uk, w_uv, w_out):
    hbm = pl.BlockSpec(memory_space=pl.ANY)
    bf16, f32 = jnp.bfloat16, jnp.float32
    dma, chunks = pltpu.SemaphoreType.DMA, len(COLUMNS)
    return pl.pallas_call(
        kernel,
        out_shape=jax.ShapeDtypeStruct((8, OUT), bf16),
        in_specs=[hbm] * 8,
        out_specs=pl.BlockSpec(memory_space=pltpu.VMEM),
        scratch_shapes=[
            pltpu.VMEM((ROWS, HEADS * NOPE), bf16),
            pltpu.VMEM((ROWS, HEADS * ROPE), bf16),
            pltpu.VMEM((ROWS, LAT), bf16),
            pltpu.VMEM((ROPE, ROWS), bf16),
            pltpu.VMEM((32, 128), jnp.int32),
            pltpu.VMEM((LAT, HEADS * NOPE), bf16),
            pltpu.VMEM((LAT, HEADS * VDIM), bf16),
            pltpu.VMEM((HEADS * VDIM, OUT), bf16),
            pltpu.VMEM((32, 8, 16, WIDE), bf16),
            pltpu.VMEM((8, 16, WIDE), bf16),
            pltpu.VMEM((HEADS * ROWS, WIDE), bf16),
            pltpu.VMEM((HEADS * ROWS, LAT), f32),
            pltpu.VMEM((HEADS * ROWS, 128), f32),
            pltpu.VMEM((HEADS * ROWS, 128), f32),
            pltpu.VMEM((ROWS, HEADS * VDIM), bf16),
            pltpu.VMEM((64, OUT), bf16),
            pltpu.VMEM((64, OUT), bf16),
            pltpu.VMEM((64, OUT), f32),
            pltpu.VMEM((64, OUT), bf16),
            pltpu.VMEM((3, 16, OUT), bf16),
            pltpu.VMEM((16, OUT), f32),
            pltpu.VMEM((16, OUT // 2), bf16),
            pltpu.VMEM((16, OUT // 2), bf16),
            dma((8,)),
            dma((7,)), dma((7,)),
            dma((2, 2)), dma((2, 2)),
            dma((8,)), dma((8,)),
            dma((GROUPS, 2)), dma((GROUPS, 2)),
            dma((GROUPS,)), dma((GROUPS,)),
            dma((GROUPS,)), dma((GROUPS,)),
            dma((chunks,)), dma((chunks,)),
            dma((chunks, 3)), dma((chunks, 3)),
            dma((chunks,)), dma((chunks,)),
        ],
        compiler_params=pltpu.CompilerParams(
            collective_id=0, has_side_effects=True, vmem_limit_bytes=VMEM_BYTES
        ),
    )(q_nope, q_rope, latent, rope_keys.T, seg_ids.reshape(32, 128), w_uk, w_uv, w_out)


def solution(mesh):
    placed = (
        P("ctx", "head"),
        P("ctx", "head"),
        P("ctx", None),
        P("ctx", None),
        P(),
        P(None, "head"),
        P(None, "head"),
        P("head", None),
    )
    return jax.shard_map(
        body, mesh=mesh, in_specs=placed, out_specs=P(("ctx", "head"), None), check_vma=False
    )
```

time: 82.7 us -> 65.7 us (0.79)
  the two profiles are of different devices: /device:TPU:80 before, /device:TPU:24 now
where the time goes in v2:
time: 65.7 us; the launch traced here: 65.6 us
  Pallas kernels  64.1 us (98%)
  local copies, waits for them, and re-layouts  1.45 us (2%)
    pallas_call x1, Pallas kernels, body(): pl.pallas_call(kernel, out_shape=jax.ShapeDtypeStruct((8, OUT), bf16), in...  64.1 us
    unnamed x1, local copies, waits for them, and re-layouts  1.45 us

profile of v2, /device:TPU:24, one launch (start us, length us, event | category | flops | bytes accessed | tf_op | source)
XLA Modules:
  0.0 65.6 jit_solution(1124268913540595926)
XLA Ops:
  0.0 64.1 %shard_map.82 = bf16[8,3584]{1,0:T(8,128)(2,1)} custom-call(bf16[128,512]{1,0:T(8,128)(2,1)} %qn_hbm.1, bf16[128,256]{1,0:T(8,128)(2,1)} %qr_hbm.1, bf16[128,512]{1,0:T(8,128)(2,1)} %lat_hbm.1, bf16[64,128]{1,0:T(8,128)(2,1)} %bitcast.2, s32[32,128]{1,0:T(8,128)} %bitcast.3, bf16[512,512]{1,0:T(8,128)(2,1)} %wuk_hbm.1, bf16[512,512]{1,0:T(8,128)(2,1)} %wuv_hbm.1, ...), custom_call_target="tpu_custom_call" | custom-call | tf_op jit(solution)/shard_map/pallas_call | solution.py:393
  64.1 1.4 %copy.10 = bf16[8,3584]{1,0:T(8,128)(2,1)} copy(bf16[8,3584]{1,0:T(8,128)(2,1)} %shard_map.82) | data formatting | bytes 114688

commit v3 on v2

--- a/solution.py
+++ b/solution.py
@@ -17,7 +17,8 @@
 HEADS = 4
 OUT = 3584
 GROUPS = 6
-COLUMNS = ((0, 1024), (1024, 1024), (2048, 1024), (3072, 512))
+COLUMNS = tuple((512 * i, 512) for i in range(7))
+TILES = 9
 VMEM_BYTES = 62 * 2**20
 MESH = pl.DeviceIdType.MESH
 NT = (((1,), (1,)), ((), ()))
@@ -37,8 +38,8 @@
 def kernel(
     qn_hbm, qr_hbm, lat_hbm, rope_hbm, seg_hbm, wuk_hbm, wuv_hbm, wout_hbm, o_ref,
     qn_ref, qr_ref, lat_ref, rope_ref, seg_ref, wuk, wuv, wout,
-    kb, kown, qb, acc, m_ref, l_ref, hob, sib_out, sib_in, own, x_out, x_in, total, z_out, z_in,
-    w_sem, zs, zr, ys, yr, ws, wr, xs, xr, rs, rr, cs, cr, rcs, rcr, rxs, rxr, rzs, rzr,
+    kb, keys_ref, kown, qb, acc, m_ref, l_ref, hob, sib_out, sib_in, own, x_out, x_in, total, z_out, z_in,
+    met, w_sem, zs, zr, ys, yr, ws, wr, xs, xr, cs, cr, rcs, rcr, rxs, rxr, rzs, rzr,
 ):
     ctx, head = lax.axis_index("ctx"), lax.axis_index("head")
     y, zlo = lax.div(ctx, 8), lax.rem(ctx, 8)
@@ -47,10 +48,10 @@
     last_row = y == 3
     other = 1 - core
     sibling = device(x, y, z, other)
-    quarter = 4 * core + x
+    half = 2 * core + lax.rem(x, 2)
 
     barrier = pltpu.get_barrier_semaphore()
-    partners = [device(x, y, z + s, core) for s in (1, 2, 3, 4, 15, 14, 13, 12, 8)]
+    partners = [device(x, y, z + s, core) for s in (1, 2, 3, 4, 15, 14, 13, 12)]
     partners += [device(x, y + s, z, core) for s in (1, 2, 3)]
     partners += [device(x + s, y, z, core) for s in (1, 2, 3)]
     partners += [sibling]
@@ -68,46 +69,59 @@
     loads[0].wait()
     loads[1].wait()
     rope = jnp.transpose(rope_ref[...].astype(jnp.float32)).astype(jnp.bfloat16)
-    kown[...] = jnp.concatenate(
+    keys_ref[...] = jnp.concatenate(
         [lat_ref[...], rope, jnp.zeros((ROWS, WIDE - LAT - ROPE), jnp.bfloat16)], axis=1
-    ).reshape(8, 16, WIDE)
+    )
+    for q in range(4):
+        for r in range(2):
+            at = 32 * q + 16 * r
+            for lane in range(4):
+                kown[q, 4 * r + lane] = lat_ref[at:at + 16, 128 * lane:128 * lane + 128]
+        kown[q, 8] = jnp.concatenate([rope[32 * q:32 * q + 16], rope[32 * q + 16:32 * q + 32]], axis=1)
 
     @pl.when(jnp.logical_not(last_row))
     def _():
-        kb[ctx, quarter] = kown[quarter]
+        kb[ctx, half] = kown[half]
 
     pl.semaphore_wait(barrier, len(partners))
+    pl.semaphore_signal(met, inc=1, device_id=device(x, y, z + 4, core), device_id_type=MESH)
 
     steps = [1, 15, 2, 14, 3, 13, 4 + 8 * core]
 
     def z_send(i):
         wanted = jnp.logical_not(last_row) | (lax.rem(zlo + steps[i], 8) > zlo)
-        return wanted, remote(
-            kown.at[quarter], kb.at[ctx, quarter], zs.at[i], zr.at[i], device(x, y, z + steps[i], core)
-        )
+        return wanted, remote(kown.at[half], kb.at[ctx, half], zs.at[i], zr.at[i], device(x, y, z + steps[i], core))
 
     def z_recv(i):
         source = lax.rem(zlo + 16 - steps[i], 8)
-        piece = kb.at[y * 8 + source, quarter]
+        piece = kb.at[y * 8 + source, half]
         return source, remote(piece, piece, zs.at[i], zr.at[i], sibling)
 
-    def y_one(block_z):
-        piece = kb.at[y * 8 + block_z, quarter]
+    def y_hop(hop, block_z):
+        piece = kb.at[y * 8 + block_z, half]
         g = lax.div(block_z, 4)
-        return remote(piece, piece, ys.at[0, g], yr.at[0, g], device(x, y + 1, z, core))
+        return remote(piece, piece, ys.at[hop - 1, g], yr.at[hop - 1, g], device(x, y + hop, z, core))
+
+    def slot(block_z):
+        return jnp.where(block_z >= zlo, 24 + block_z, block_z)
 
     def y_three(block_z):
         return remote(
-            kb.at[block_z, quarter], kb.at[24 + block_z, quarter], ws.at[block_z], wr.at[block_z],
-            device(x, 3, z, core),
+            kb.at[block_z, half], kb.at[slot(block_z), half], ws.at[block_z], wr.at[block_z], device(x, 3, z, core)
         )
 
-    def y_group(hop, g, row):
-        piece = kb.at[pl.ds(row * 8 + 4 * g, 4), quarter]
-        return remote(piece, piece, ys.at[hop - 1, g], yr.at[hop - 1, g], device(x, y + hop, z, core))
-
-    onward, back = jnp.where(core == 0, 1, 3), jnp.where(core == 0, 3, 1)
-    sides = (onward, back)
+    def y_back(block_z):
+        g = lax.div(block_z, 4)
+        return remote(
+            kb.at[slot(block_z), half], kb.at[block_z, half], ys.at[1, g], yr.at[1, g], device(x, 2, z, core)
+        )
+
+    def y_group(k, g, row):
+        piece = kb.at[pl.ds(row * 8 + 4 * g, 4), half]
+        return remote(piece, piece, ys.at[k - 1, g], yr.at[k - 1, g], sibling)
+
+    sides = (jnp.where(core == 0, 1, 3), jnp.where(core == 0, 3, 1))
+    parts_of = (pl.ds(0, 4), pl.ds(4, 5))
 
     def place_of(i):
         k, g = lax.div(i, 2), lax.rem(i, 2)
@@ -118,20 +132,16 @@
         return (y >= k) & ((k > 0) | last_row | (zlo > 4 * g))
 
     def x_one(block_z, side):
-        piece = kb.at[y * 8 + block_z, quarter]
+        piece = kb.at[y * 8 + block_z, half, parts_of[side]]
         g = lax.div(block_z, 4)
         return remote(piece, piece, xs.at[g, side], xr.at[g, side], device(x + sides[side], y, z, core))
 
     def x_group(i, side):
-        piece = kb.at[pl.ds(place_of(i), 4), quarter]
+        piece = kb.at[pl.ds(place_of(i), 4), half, parts_of[side]]
         return remote(piece, piece, xs.at[i, side], xr.at[i, side], device(x + sides[side], y, z, core))
 
-    def x_pass(i):
-        piece = kb.at[pl.ds(place_of(i), 4), 4 * core + lax.rem(x + back, 4)]
-        return remote(piece, piece, rs.at[i], rr.at[i], device(x + onward, y, z, core))
-
     def core_copy(i):
-        piece = kb.at[pl.ds(place_of(i), 4), pl.ds(4 * core, 4)]
+        piece = kb.at[pl.ds(place_of(i), 4), pl.ds(2 * core, 2)]
         return remote(piece, piece, cs.at[i], cr.at[i], sibling)
 
     def x_start(block_z):
@@ -141,13 +151,23 @@
             x_one(block_z, 1).start()
 
     def forward(block_z):
+        @pl.when(y == 0)
+        def _():
+            y_three(block_z).start()
+
         @pl.when(jnp.logical_not(last_row))
         def _():
-            y_one(block_z).start()
-
-        @pl.when((y == 0) & (block_z >= zlo))
-        def _():
-            y_three(block_z).start()
+            y_hop(1, block_z).start()
+
+        @pl.when(y == 1)
+        def _():
+            y_hop(2, block_z).start()
+
+    def pass_back(block_z):
+        @pl.when(last_row)
+        def _():
+            y_three(block_z).wait_recv()
+            y_back(block_z).start()
 
     for i in range(7):
         wanted, copy = z_send(i)
@@ -160,16 +180,13 @@
         absorbed = lax.dot_general(
             qn_ref[:, h * NOPE:(h + 1) * NOPE], wuk[:, h * NOPE:(h + 1) * NOPE], NT, preferred_element_type=jnp.float32
         ).astype(jnp.bfloat16)
-        tail = jnp.concatenate(
-            [qr_ref[:, h * ROPE:(h + 1) * ROPE], jnp.zeros((ROWS, WIDE - LAT - ROPE), jnp.bfloat16)], axis=1
-        )
-        qb[h * ROWS:(h + 1) * ROWS, :LAT] = absorbed
-        qb[h * ROWS:(h + 1) * ROWS, LAT:] = tail
-
-    @pl.when(last_row)
-    def _():
-        y_three(zlo).wait_recv()
-
+        rows = slice(h * ROWS, (h + 1) * ROWS)
+        tail = qr_ref[:, h * ROPE:(h + 1) * ROPE]
+        for r in range(2):
+            qb[r, rows, :LAT] = absorbed
+            qb[r, rows, LAT:] = jnp.concatenate([jnp.zeros_like(tail)] * r + [tail] + [jnp.zeros_like(tail)] * (1 - r), axis=1)
+
+    pass_back(zlo)
     x_start(zlo)
     for i in range(7):
         source, copy = z_recv(i)
@@ -178,17 +195,9 @@
         def _():
             copy.wait_recv()
 
-        @pl.when(last_row & (source > zlo))
-        def _():
-            y_three(source).wait_recv()
-
         forward(source)
+        pass_back(source)
         x_start(source)
-
-    for g in range(2):
-        @pl.when(y < 2)
-        def _():
-            y_group(2, g, y).start()
 
     loads[5].wait()
     seg = seg_ref[...]
@@ -204,11 +213,11 @@
     first2 = jnp.concatenate([first, first], axis=0)
     factor = math.log2(math.e) / math.sqrt(NOPE + ROPE)
 
-    keys = kown[...].reshape(ROWS, WIDE)
+    keys = keys_ref[...]
     diagonal = (across <= down) & (across + ctx * ROWS >= first)
     for h in range(HEADS):
         rows = slice(h * ROWS, (h + 1) * ROWS)
-        scores = lax.dot_general(qb[rows, :], keys, NT, preferred_element_type=jnp.float32) * factor
+        scores = lax.dot_general(qb[0, rows, :], keys, NT, preferred_element_type=jnp.float32) * factor
         scores = jnp.where(diagonal, scores, -jnp.inf)
         top = jnp.broadcast_to(jnp.max(scores, axis=1, keepdims=True), (ROWS, 128))
         powers = jnp.exp2(scores - top)
@@ -225,31 +234,49 @@
             x_group(i, 0).start()
             x_group(i, 1).start()
 
-    def stage_pass(i):
+    def stage_core(i):
         @pl.when((i < GROUPS) & needed(i))
         def _():
             x_group(i, 0).wait_recv()
-            x_pass(i).start()
-
-    def stage_core(i):
-        @pl.when((i >= 0) & (i < GROUPS) & needed(i))
-        def _():
             x_group(i, 1).wait_recv()
-            x_pass(i).wait_recv()
             core_copy(i).start()
+
+    column = lax.broadcasted_iota(jnp.int32, (1, 512), 1)
+    within = (
+        lax.rem(lax.div(column, 64), 4) * 128
+        + lax.rem(lax.div(column, 16), 4) * 32
+        + lax.div(column, 256) * 16
+        + lax.rem(column, 16)
+    )
 
     def stage_attend(i):
         @pl.when((i >= 0) & needed(i))
         def _():
             core_copy(i).wait_recv()
             begin = place_of(i)
-            block = kb[pl.ds(begin, 4)].reshape(512, WIDE)
-            place = begin * ROWS + lax.broadcasted_iota(jnp.int32, (256, 512), 1)
+            some = pl.ds(begin, 4)
+            lats = [
+                jnp.concatenate([kb[some, :, 4 * r + lane].reshape(256, 128) for lane in range(4)], axis=1)
+                for r in range(2)
+            ]
+            ropes = kb[some, :, 8].reshape(256, 128)
+            values = jnp.concatenate(lats, axis=0)
+            place = begin * ROWS + within
             place = jnp.where(last_row & (place >= ctx * ROWS), place - 24 * ROWS, place)
-            visible = (place >= first2) & (place < ctx * ROWS)
-            for half in range(2):
-                rows = slice(half * 256, (half + 1) * 256)
-                scores = lax.dot_general(qb[rows, :], block, NT, preferred_element_type=jnp.float32) * factor
+            place = jnp.where(place < ctx * ROWS, place, -1)
+            visible = place >= first2
+            for part in range(2):
+                rows = slice(part * 256, (part + 1) * 256)
+                scores = jnp.concatenate(
+                    [
+                        lax.dot_general(
+                            qb[r, rows, :], jnp.concatenate([lats[r], ropes], axis=1), NT,
+                            preferred_element_type=jnp.float32,
+                        )
+                        for r in range(2)
+                    ],
+                    axis=1,
+                ) * factor
                 scores = jnp.where(visible, scores, -jnp.inf)
                 before = m_ref[rows, :]
                 top = jnp.maximum(before, jnp.max(scores, axis=1, keepdims=True))
@@ -260,17 +287,16 @@
                     (powers[:, :128] + powers[:, 128:256]) + (powers[:, 256:384] + powers[:, 384:])
                 )
                 acc[rows, :] = acc[rows, :] * jnp.concatenate([shrink] * 4, axis=1) + jnp.dot(
-                    powers.astype(jnp.bfloat16), block[:, :LAT], preferred_element_type=jnp.float32
+                    powers.astype(jnp.bfloat16), values, preferred_element_type=jnp.float32
                 )
 
     def step(t, carry):
         stage_x(t + 2)
-        stage_pass(t)
-        stage_core(t - 1)
-        stage_attend(t - 2)
+        stage_core(t)
+        stage_attend(t - 1)
         return carry
 
-    lax.fori_loop(0, GROUPS + 2, step, 0)
+    lax.fori_loop(0, GROUPS + 1, step, 0)
 
     loads[6].wait()
     parts = []
@@ -316,20 +342,23 @@
     theirs = hob[pl.ds(pl.multiple_of(64 * other, 64), 64), :]
     mine = hob[pl.ds(pl.multiple_of(64 * core, 64), 64), :]
     swapped = jnp.concatenate([theirs, mine], axis=0)
-    for j, (begin, width) in enumerate(COLUMNS):
-        columns = slice(begin, begin + width)
-        part = jnp.dot(swapped, wout[:, columns], preferred_element_type=jnp.float32)
-        sib_out[:, columns] = part[:64].astype(jnp.bfloat16)
-        rc_copy(j).start()
-        own[:, columns] = part[64:]
-    for j, (begin, width) in enumerate(COLUMNS):
-        columns = slice(begin, begin + width)
-        rc_copy(j).wait_recv()
-        part = own[:, columns] + sib_in[:, columns].astype(jnp.float32)
-        own[:, columns] = part
-        x_out[:, columns] = part.astype(jnp.bfloat16)
-        for copy in rx_copies(j):
-            copy.start()
+    chunks = len(COLUMNS)
+    for j in range(chunks + 2):
+        if j < chunks:
+            columns = slice(COLUMNS[j][0], sum(COLUMNS[j]))
+            part = jnp.dot(swapped, wout[:, columns], preferred_element_type=jnp.float32)
+            sib_out[:, columns] = part[:64].astype(jnp.bfloat16)
+            rc_copy(j).start()
+            own[:, columns] = part[64:]
+        if j >= 2:
+            columns = slice(COLUMNS[j - 2][0], sum(COLUMNS[j - 2]))
+            rc_copy(j - 2).wait_recv()
+            part = own[:, columns] + sib_in[:, columns].astype(jnp.float32)
+            own[:, columns] = part
+            x_out[:, columns] = part.astype(jnp.bfloat16)
+            for copy in rx_copies(j - 2):
+                copy.start()
+    pl.semaphore_wait(met, 1)
     for j, (begin, width) in enumerate(COLUMNS):
         columns = slice(begin, begin + width)
         for copy in rx_copies(j):
@@ -339,16 +368,16 @@
             part = part + x_in[s, :, columns].astype(jnp.float32)
         total[:, columns] = part
         away = total[pl.ds(pl.multiple_of(8 - 8 * zhi, 8), 8), columns]
-        half = width // 2
-        z_out[:, begin // 2:begin // 2 + half] = jnp.concatenate([away[:, :half], away[:, half:]], axis=0).astype(
+        wide = width // 2
+        z_out[:, begin // 2:begin // 2 + wide] = jnp.concatenate([away[:, :wide], away[:, wide:]], axis=0).astype(
             jnp.bfloat16
         )
         rz_copy(j).start()
     for j, (begin, width) in enumerate(COLUMNS):
         columns = slice(begin, begin + width)
-        half = width // 2
+        wide = width // 2
         rz_copy(j).wait_recv()
-        came = z_in[:, begin // 2:begin // 2 + half].astype(jnp.float32)
+        came = z_in[:, begin // 2:begin // 2 + wide].astype(jnp.float32)
         came = jnp.concatenate([came[:8], came[8:]], axis=1)
         o_ref[:, columns] = (total[pl.ds(pl.multiple_of(8 * zhi, 8), 8), columns] + came).astype(jnp.bfloat16)
 
@@ -356,7 +385,7 @@
         wanted, copy = z_send(i)
         pl.when(wanted)(copy.wait_send)
     for block_z in range(8):
-        @pl.when((y == 0) & (block_z >= zlo))
+        @pl.when(y == 0)
         def _():
             y_three(block_z).wait_send()
     for g in range(2):
@@ -364,7 +393,7 @@
         def _():
             y_group(1, g, y).wait_send()
 
-        @pl.when(y < 2)
+        @pl.when((y == 1) | last_row)
         def _():
             y_group(2, g, y).wait_send()
 
@@ -373,7 +402,6 @@
         def _():
             x_group(i, 0).wait_send()
             x_group(i, 1).wait_send()
-            x_pass(i).wait_send()
             core_copy(i).wait_send()
 
         return carry
@@ -404,9 +432,10 @@
             pltpu.VMEM((LAT, HEADS * NOPE), bf16),
             pltpu.VMEM((LAT, HEADS * VDIM), bf16),
             pltpu.VMEM((HEADS * VDIM, OUT), bf16),
-            pltpu.VMEM((32, 8, 16, WIDE), bf16),
-            pltpu.VMEM((8, 16, WIDE), bf16),
-            pltpu.VMEM((HEADS * ROWS, WIDE), bf16),
+            pltpu.VMEM((32, 4, TILES, 16, 128), bf16),
+            pltpu.VMEM((ROWS, WIDE), bf16),
+            pltpu.VMEM((4, TILES, 16, 128), bf16),
+            pltpu.VMEM((2, HEADS * ROWS, WIDE), bf16),
             pltpu.VMEM((HEADS * ROWS, LAT), f32),
             pltpu.VMEM((HEADS * ROWS, 128), f32),
             pltpu.VMEM((HEADS * ROWS, 128), f32),
@@ -419,12 +448,12 @@
             pltpu.VMEM((16, OUT), f32),
             pltpu.VMEM((16, OUT // 2), bf16),
             pltpu.VMEM((16, OUT // 2), bf16),
+            pltpu.SemaphoreType.REGULAR,
             dma((8,)),
             dma((7,)), dma((7,)),
             dma((2, 2)), dma((2, 2)),
             dma((8,)), dma((8,)),
             dma((GROUPS, 2)), dma((GROUPS, 2)),
-            dma((GROUPS,)), dma((GROUPS,)),
             dma((GROUPS,)), dma((GROUPS,)),
             dma((chunks,)), dma((chunks,)),
             dma((chunks, 3)), dma((chunks, 3)),

time: 65.7 us -> 61.7 us (0.939)
  Pallas kernels: 64.1 us -> 60.1 us
    pallas_call x1, Pallas kernels: 64.1 us -> 60.1 us  [body(): pl.pallas_call(kernel, out_shape=jax.ShapeDtypeStruct((8, OUT), bf16), in...]
where the time goes in v3:
time: 61.7 us; the launch traced here: 61.5 us
  Pallas kernels  60.1 us (97%)
  local copies, waits for them, and re-layouts  1.45 us (2%)
    pallas_call x1, Pallas kernels, body(): pl.pallas_call(kernel, out_shape=jax.ShapeDtypeStruct((8, OUT), bf16), in...  60.1 us
    unnamed x1, local copies, waits for them, and re-layouts  1.45 us

profile of v3, /device:TPU:24, one launch (start us, length us, event | category | flops | bytes accessed | tf_op | source)
XLA Modules:
  0.0 61.5 jit_solution(3182624768759623671)
XLA Ops:
  0.0 60.1 %shard_map.82 = bf16[8,3584]{1,0:T(8,128)(2,1)} custom-call(bf16[128,512]{1,0:T(8,128)(2,1)} %qn_hbm.1, bf16[128,256]{1,0:T(8,128)(2,1)} %qr_hbm.1, bf16[128,512]{1,0:T(8,128)(2,1)} %lat_hbm.1, bf16[64,128]{1,0:T(8,128)(2,1)} %bitcast.2, s32[32,128]{1,0:T(8,128)} %bitcast.3, bf16[512,512]{1,0:T(8,128)(2,1)} %wuk_hbm.1, bf16[512,512]{1,0:T(8,128)(2,1)} %wuv_hbm.1, ...), custom_call_target="tpu_custom_call" | custom-call | tf_op jit(solution)/shard_map/pallas_call | solution.py:421
  60.1 1.4 %copy.10 = bf16[8,3584]{1,0:T(8,128)(2,1)} copy(bf16[8,3584]{1,0:T(8,128)(2,1)} %shard_map.82) | data formatting | bytes 114688

commit v4 on v3

--- a/solution.py
+++ b/solution.py
@@ -19,6 +19,7 @@
 GROUPS = 6
 COLUMNS = tuple((512 * i, 512) for i in range(7))
 TILES = 9
+OWN = 2
 VMEM_BYTES = 62 * 2**20
 MESH = pl.DeviceIdType.MESH
 NT = (((1,), (1,)), ((), ()))
@@ -81,39 +82,50 @@
 
     @pl.when(jnp.logical_not(last_row))
     def _():
-        kb[ctx, half] = kown[half]
+        kb[8 * y + OWN, half] = kown[half]
 
     pl.semaphore_wait(barrier, len(partners))
+
     pl.semaphore_signal(met, inc=1, device_id=device(x, y, z + 4, core), device_id_type=MESH)
 
     steps = [1, 15, 2, 14, 3, 13, 4 + 8 * core]
+
+    slots = [1, 3, 0, 4, 7, 5, 6]
+
+    def block_z(slot):
+        return lax.rem(slot + zlo + 8 - OWN, 8)
 
     def z_send(i):
         wanted = jnp.logical_not(last_row) | (lax.rem(zlo + steps[i], 8) > zlo)
-        return wanted, remote(kown.at[half], kb.at[ctx, half], zs.at[i], zr.at[i], device(x, y, z + steps[i], core))
+        return wanted, remote(
+            kown.at[half], kb.at[8 * y + slots[i], half], zs.at[i], zr.at[i], device(x, y, z + steps[i], core)
+        )
+
+    def z_start(i):
+        wanted, copy = z_send(i)
+        pl.when(wanted)(copy.start)
 
     def z_recv(i):
-        source = lax.rem(zlo + 16 - steps[i], 8)
-        piece = kb.at[y * 8 + source, half]
-        return source, remote(piece, piece, zs.at[i], zr.at[i], sibling)
-
-    def y_hop(hop, block_z):
-        piece = kb.at[y * 8 + block_z, half]
-        g = lax.div(block_z, 4)
+        piece = kb.at[8 * y + slots[i], half]
+        return remote(piece, piece, zs.at[i], zr.at[i], sibling)
+
+    def y_hop(hop, slot):
+        piece = kb.at[y * 8 + slot, half]
+        g = slot // 4
         return remote(piece, piece, ys.at[hop - 1, g], yr.at[hop - 1, g], device(x, y + hop, z, core))
 
-    def slot(block_z):
-        return jnp.where(block_z >= zlo, 24 + block_z, block_z)
-
-    def y_three(block_z):
+    def place_in_last(slot):
+        return jnp.where(block_z(slot) >= zlo, 24 + slot, slot)
+
+    def y_three(slot):
         return remote(
-            kb.at[block_z, half], kb.at[slot(block_z), half], ws.at[block_z], wr.at[block_z], device(x, 3, z, core)
+            kb.at[slot, half], kb.at[place_in_last(slot), half], ws.at[slot], wr.at[slot], device(x, 3, z, core)
         )
 
-    def y_back(block_z):
-        g = lax.div(block_z, 4)
+    def y_back(slot):
+        g = slot // 4
         return remote(
-            kb.at[slot(block_z), half], kb.at[block_z, half], ys.at[1, g], yr.at[1, g], device(x, 2, z, core)
+            kb.at[place_in_last(slot), half], kb.at[slot, half], ys.at[1, g], yr.at[1, g], device(x, 2, z, core)
         )
 
     def y_group(k, g, row):
@@ -124,17 +136,11 @@
     parts_of = (pl.ds(0, 4), pl.ds(4, 5))
 
     def place_of(i):
-        k, g = lax.div(i, 2), lax.rem(i, 2)
-        return (y - k) * 8 + 4 * g
+        return (y - lax.rem(i, 3)) * 8 + 4 * lax.div(i, 3)
 
     def needed(i):
-        k, g = lax.div(i, 2), lax.rem(i, 2)
-        return (y >= k) & ((k > 0) | last_row | (zlo > 4 * g))
-
-    def x_one(block_z, side):
-        piece = kb.at[y * 8 + block_z, half, parts_of[side]]
-        g = lax.div(block_z, 4)
-        return remote(piece, piece, xs.at[g, side], xr.at[g, side], device(x + sides[side], y, z, core))
+        k, g = lax.rem(i, 3), lax.div(i, 3)
+        return (y >= k) & ((k > 0) | last_row | (zlo >= 1 + 2 * g))
 
     def x_group(i, side):
         piece = kb.at[pl.ds(place_of(i), 4), half, parts_of[side]]
@@ -144,39 +150,38 @@
         piece = kb.at[pl.ds(place_of(i), 4), pl.ds(2 * core, 2)]
         return remote(piece, piece, cs.at[i], cr.at[i], sibling)
 
-    def x_start(block_z):
-        @pl.when(last_row | (zlo > 4 * lax.div(block_z, 4)))
-        def _():
-            x_one(block_z, 0).start()
-            x_one(block_z, 1).start()
-
-    def forward(block_z):
+    def forward(slot):
         @pl.when(y == 0)
         def _():
-            y_three(block_z).start()
+            y_three(slot).start()
 
         @pl.when(jnp.logical_not(last_row))
         def _():
-            y_hop(1, block_z).start()
+            y_hop(1, slot).start()
 
         @pl.when(y == 1)
         def _():
-            y_hop(2, block_z).start()
-
-    def pass_back(block_z):
+            y_hop(2, slot).start()
+
+    def pass_back(slot):
         @pl.when(last_row)
         def _():
-            y_three(block_z).wait_recv()
-            y_back(block_z).start()
-
-    for i in range(7):
-        wanted, copy = z_send(i)
-        pl.when(wanted)(copy.start)
-    forward(zlo)
+            y_three(slot).wait_recv()
+            y_back(slot).start()
+
+    z_start(0)
+    z_start(1)
+    forward(OWN)
 
     for load in loads[2:5]:
         load.wait()
     for h in range(HEADS):
+        if h:
+            if h < 3:
+                z_start(2 * h)
+                z_start(2 * h + 1)
+            else:
+                z_start(6)
         absorbed = lax.dot_general(
             qn_ref[:, h * NOPE:(h + 1) * NOPE], wuk[:, h * NOPE:(h + 1) * NOPE], NT, preferred_element_type=jnp.float32
         ).astype(jnp.bfloat16)
@@ -186,18 +191,30 @@
             qb[r, rows, :LAT] = absorbed
             qb[r, rows, LAT:] = jnp.concatenate([jnp.zeros_like(tail)] * r + [tail] + [jnp.zeros_like(tail)] * (1 - r), axis=1)
 
-    pass_back(zlo)
-    x_start(zlo)
-    for i in range(7):
-        source, copy = z_recv(i)
-
-        @pl.when(jnp.logical_not(last_row) | (source < zlo))
-        def _():
-            copy.wait_recv()
-
-        forward(source)
-        pass_back(source)
-        x_start(source)
+    def arrive(i):
+        @pl.when(jnp.logical_not(last_row) | (block_z(slots[i]) < zlo))
+        def _():
+            z_recv(i).wait_recv()
+
+        forward(slots[i])
+        pass_back(slots[i])
+
+    def stage_x(i):
+        k, g = lax.rem(i, 3), lax.div(i, 3)
+
+        @pl.when((i < GROUPS) & needed(i))
+        def _():
+            @pl.when(k > 0)
+            def _():
+                y_group(jnp.maximum(k, 1), g, y - k).wait_recv()
+
+            x_group(i, 0).start()
+            x_group(i, 1).start()
+
+    pass_back(OWN)
+    for i in range(3):
+        arrive(i)
+    stage_x(0)
 
     loads[5].wait()
     seg = seg_ref[...]
@@ -210,7 +227,7 @@
     down = lax.broadcasted_iota(jnp.int32, (ROWS, ROWS), 0)
     across = lax.broadcasted_iota(jnp.int32, (ROWS, ROWS), 1)
     first = jnp.sum(jnp.where(down == across, first, 0.0), axis=1, keepdims=True).astype(jnp.int32)
-    first2 = jnp.concatenate([first, first], axis=0)
+    first2 = jnp.concatenate([first] * HEADS, axis=0)
     factor = math.log2(math.e) / math.sqrt(NOPE + ROPE)
 
     keys = keys_ref[...]
@@ -225,14 +242,18 @@
         l_ref[rows, :] = powers
         acc[rows, :] = jnp.dot(powers.astype(jnp.bfloat16), keys[:, :LAT], preferred_element_type=jnp.float32)
 
-    def stage_x(i):
-        k, g = lax.div(i, 2), lax.rem(i, 2)
-
-        @pl.when((i < GROUPS) & needed(i))
-        def _():
-            y_group(k, g, y - k).wait_recv()
-            x_group(i, 0).start()
-            x_group(i, 1).start()
+    @pl.when(last_row)
+    def _():
+        stage_x(1)
+        stage_x(2)
+
+    for i in range(3, 7):
+        arrive(i)
+
+    @pl.when(jnp.logical_not(last_row))
+    def _():
+        stage_x(1)
+        stage_x(2)
 
     def stage_core(i):
         @pl.when((i < GROUPS) & needed(i))
@@ -242,15 +263,15 @@
             core_copy(i).start()
 
     column = lax.broadcasted_iota(jnp.int32, (1, 512), 1)
+    beside = lax.rem(lax.div(column, 64), 4)
     within = (
-        lax.rem(lax.div(column, 64), 4) * 128
-        + lax.rem(lax.div(column, 16), 4) * 32
+        lax.rem(lax.div(column, 16), 4) * 32
         + lax.div(column, 256) * 16
         + lax.rem(column, 16)
     )
 
     def stage_attend(i):
-        @pl.when((i >= 0) & needed(i))
+        @pl.when((i >= 0) & needed(jnp.maximum(i, 0)))
         def _():
             core_copy(i).wait_recv()
             begin = place_of(i)
@@ -261,12 +282,12 @@
             ]
             ropes = kb[some, :, 8].reshape(256, 128)
             values = jnp.concatenate(lats, axis=0)
-            place = begin * ROWS + within
+            place = (y - lax.rem(i, 3)) * 1024 + block_z(4 * lax.div(i, 3) + beside) * ROWS + within
             place = jnp.where(last_row & (place >= ctx * ROWS), place - 24 * ROWS, place)
             place = jnp.where(place < ctx * ROWS, place, -1)
             visible = place >= first2
-            for part in range(2):
-                rows = slice(part * 256, (part + 1) * 256)
+            for part in range(1):
+                rows = slice(part * 512, (part + 1) * 512)
                 scores = jnp.concatenate(
                     [
                         lax.dot_general(
@@ -291,8 +312,8 @@
                 )
 
     def step(t, carry):
-        stage_x(t + 2)
         stage_core(t)
+        stage_x(t + 3)
         stage_attend(t - 1)
         return carry
 
@@ -384,10 +405,10 @@
     for i in range(7):
         wanted, copy = z_send(i)
         pl.when(wanted)(copy.wait_send)
-    for block_z in range(8):
+    for slot in range(8):
         @pl.when(y == 0)
         def _():
-            y_three(block_z).wait_send()
+            y_three(slot).wait_send()
     for g in range(2):
         @pl.when(jnp.logical_not(last_row))
         def _():

time: 61.7 us -> 60.1 us (0.974)
  Pallas kernels: 60.1 us -> 58.2 us
    pallas_call x1, Pallas kernels: 60.1 us -> 58.2 us  [body(): pl.pallas_call(kernel, out_shape=jax.ShapeDtypeStruct((8, OUT), bf16), in...]
where the time goes in v4:
time: 60.1 us; the launch traced here: 59.7 us
  Pallas kernels  58.2 us (97%)
  local copies, waits for them, and re-layouts  1.45 us (2%)
    pallas_call x1, Pallas kernels, body(): pl.pallas_call(kernel, out_shape=jax.ShapeDtypeStruct((8, OUT), bf16), in...  58.2 us
    unnamed x1, local copies, waits for them, and re-layouts  1.45 us

profile of v4, /device:TPU:24, one launch (start us, length us, event | category | flops | bytes accessed | tf_op | source)
XLA Modules:
  0.0 59.7 jit_solution(13688197727187470113)
XLA Ops:
  0.0 58.2 %shard_map.82 = bf16[8,3584]{1,0:T(8,128)(2,1)} custom-call(bf16[128,512]{1,0:T(8,128)(2,1)} %qn_hbm.1, bf16[128,256]{1,0:T(8,128)(2,1)} %qr_hbm.1, bf16[128,512]{1,0:T(8,128)(2,1)} %lat_hbm.1, bf16[64,128]{1,0:T(8,128)(2,1)} %bitcast.2, s32[32,128]{1,0:T(8,128)} %bitcast.3, bf16[512,512]{1,0:T(8,128)(2,1)} %wuk_hbm.1, bf16[512,512]{1,0:T(8,128)(2,1)} %wuv_hbm.1, ...), custom_call_target="tpu_custom_call" | custom-call | tf_op jit(solution)/shard_map/pallas_call | solution.py:442
  58.3 1.4 %copy.10 = bf16[8,3584]{1,0:T(8,128)(2,1)} copy(bf16[8,3584]{1,0:T(8,128)(2,1)} %shard_map.82) | data formatting | bytes 114688

commit v5 on v4

--- a/solution.py
+++ b/solution.py
@@ -146,9 +146,9 @@
         piece = kb.at[pl.ds(place_of(i), 4), half, parts_of[side]]
         return remote(piece, piece, xs.at[i, side], xr.at[i, side], device(x + sides[side], y, z, core))
 
-    def core_copy(i):
-        piece = kb.at[pl.ds(place_of(i), 4), pl.ds(2 * core, 2)]
-        return remote(piece, piece, cs.at[i], cr.at[i], sibling)
+    def core_copy(i, got):
+        piece = kb.at[pl.ds(place_of(i), 4), half + got * (1 - 2 * lax.rem(x, 2))]
+        return remote(piece, piece, cs.at[i, got], cr.at[i, got], sibling)
 
     def forward(slot):
         @pl.when(y == 0)
@@ -210,6 +210,7 @@
 
             x_group(i, 0).start()
             x_group(i, 1).start()
+            core_copy(i, 0).start()
 
     pass_back(OWN)
     for i in range(3):
@@ -260,7 +261,7 @@
         def _():
             x_group(i, 0).wait_recv()
             x_group(i, 1).wait_recv()
-            core_copy(i).start()
+            core_copy(i, 1).start()
 
     column = lax.broadcasted_iota(jnp.int32, (1, 512), 1)
     beside = lax.rem(lax.div(column, 64), 4)
@@ -273,7 +274,8 @@
     def stage_attend(i):
         @pl.when((i >= 0) & needed(jnp.maximum(i, 0)))
         def _():
-            core_copy(i).wait_recv()
+            core_copy(i, 0).wait_recv()
+            core_copy(i, 1).wait_recv()
             begin = place_of(i)
             some = pl.ds(begin, 4)
             lats = [
@@ -311,20 +313,35 @@
                     powers.astype(jnp.bfloat16), values, preferred_element_type=jnp.float32
                 )
 
+    plan = (
+        (0, stage_x, 3),
+        (0, stage_x, 4),
+        (0, stage_core, 0),
+        (0, stage_core, 1),
+        (0, stage_x, 5),
+        (0, stage_core, 2),
+        (1, stage_core, 3),
+        (2, stage_core, 4),
+        (3, stage_core, 5),
+    )
+
     def step(t, carry):
-        stage_core(t)
-        stage_x(t + 3)
-        stage_attend(t - 1)
+        for turn, stage, item in plan:
+            @pl.when(t == turn)
+            def _():
+                stage(item)
+
+        stage_attend(t)
         return carry
 
-    lax.fori_loop(0, GROUPS + 1, step, 0)
+    lax.fori_loop(0, GROUPS, step, 0)
 
     loads[6].wait()
     parts = []
     for h in range(HEADS):
         rows = slice(h * ROWS, (h + 1) * ROWS)
-        sums = jnp.sum(l_ref[rows, :], axis=1, keepdims=True)
-        context = (acc[rows, :] / sums).astype(jnp.bfloat16)
+        share = 1.0 / jnp.sum(l_ref[rows, :], axis=1, keepdims=True)
+        context = (acc[rows, :] * share).astype(jnp.bfloat16)
         parts.append(jnp.dot(context, wuv[:, h * VDIM:(h + 1) * VDIM], preferred_element_type=jnp.float32))
     head_out = jnp.concatenate(parts, axis=1)
     order = [32 * i + 16 * j + 8 * c for c in range(2) for i in range(4) for j in range(2)]
@@ -394,6 +411,38 @@
             jnp.bfloat16
         )
         rz_copy(j).start()
+    for i in range(7):
+        wanted, copy = z_send(i)
+        pl.when(wanted)(copy.wait_send)
+    for slot in range(8):
+        @pl.when(y == 0)
+        def _():
+            y_three(slot).wait_send()
+    for g in range(2):
+        @pl.when(jnp.logical_not(last_row))
+        def _():
+            y_group(1, g, y).wait_send()
+
+        @pl.when((y == 1) | last_row)
+        def _():
+            y_group(2, g, y).wait_send()
+
+    def drain(i, carry):
+        @pl.when(needed(i))
+        def _():
+            x_group(i, 0).wait_send()
+            x_group(i, 1).wait_send()
+            core_copy(i, 0).wait_send()
+            core_copy(i, 1).wait_send()
+
+        return carry
+
+    lax.fori_loop(0, GROUPS, drain, 0)
+    for j in range(len(COLUMNS)):
+        rc_copy(j).wait_send()
+        for copy in rx_copies(j):
+            copy.wait_send()
+
     for j, (begin, width) in enumerate(COLUMNS):
         columns = slice(begin, begin + width)
         wide = width // 2
@@ -402,36 +451,7 @@
         came = jnp.concatenate([came[:8], came[8:]], axis=1)
         o_ref[:, columns] = (total[pl.ds(pl.multiple_of(8 * zhi, 8), 8), columns] + came).astype(jnp.bfloat16)
 
-    for i in range(7):
-        wanted, copy = z_send(i)
-        pl.when(wanted)(copy.wait_send)
-    for slot in range(8):
-        @pl.when(y == 0)
-        def _():
-            y_three(slot).wait_send()
-    for g in range(2):
-        @pl.when(jnp.logical_not(last_row))
-        def _():
-            y_group(1, g, y).wait_send()
-
-        @pl.when((y == 1) | last_row)
-        def _():
-            y_group(2, g, y).wait_send()
-
-    def drain(i, carry):
-        @pl.when(needed(i))
-        def _():
-            x_group(i, 0).wait_send()
-            x_group(i, 1).wait_send()
-            core_copy(i).wait_send()
-
-        return carry
-
-    lax.fori_loop(0, GROUPS, drain, 0)
     for j in range(len(COLUMNS)):
-        rc_copy(j).wait_send()
-        for copy in rx_copies(j):
-            copy.wait_send()
         rz_copy(j).wait_send()
 
 
@@ -475,7 +495,7 @@
             dma((2, 2)), dma((2, 2)),
             dma((8,)), dma((8,)),
             dma((GROUPS, 2)), dma((GROUPS, 2)),
-            dma((GROUPS,)), dma((GROUPS,)),
+            dma((GROUPS, 2)), dma((GROUPS, 2)),
             dma((chunks,)), dma((chunks,)),
             dma((chunks, 3)), dma((chunks, 3)),
             dma((chunks,)), dma((chunks,)),

time: 60.1 us -> 59.8 us (level)
  no operation moved by 1% of the time
where the time goes in v5:
time: 59.8 us; the launch traced here: 59.4 us
  Pallas kernels  58 us (97%)
  local copies, waits for them, and re-layouts  1.45 us (2%)
    pallas_call x1, Pallas kernels, body(): pl.pallas_call(kernel, out_shape=jax.ShapeDtypeStruct((8, OUT), bf16), in...  58 us
    unnamed x1, local copies, waits for them, and re-layouts  1.45 us

profile of v5, /device:TPU:24, one launch (start us, length us, event | category | flops | bytes accessed | tf_op | source)
XLA Modules:
  0.0 59.4 jit_solution(17172835856259238989)
XLA Ops:
  0.0 58.0 %shard_map.82 = bf16[8,3584]{1,0:T(8,128)(2,1)} custom-call(bf16[128,512]{1,0:T(8,128)(2,1)} %qn_hbm.1, bf16[128,256]{1,0:T(8,128)(2,1)} %qr_hbm.1, bf16[128,512]{1,0:T(8,128)(2,1)} %lat_hbm.1, bf16[64,128]{1,0:T(8,128)(2,1)} %bitcast.2, s32[32,128]{1,0:T(8,128)} %bitcast.3, bf16[512,512]{1,0:T(8,128)(2,1)} %wuk_hbm.1, bf16[512,512]{1,0:T(8,128)(2,1)} %wuv_hbm.1, ...), custom_call_target="tpu_custom_call" | custom-call | tf_op jit(solution)/shard_map/pallas_call | solution.py:462
  58.0 1.4 %copy.10 = bf16[8,3584]{1,0:T(8,128)(2,1)} copy(bf16[8,3584]{1,0:T(8,128)(2,1)} %shard_map.82) | data formatting | bytes 114688
